TPU v7x, 128 devices: a whole 4x4x4 slice. The times are simulated.
128 devices in a mesh: lat: 4 (over y_hi, core), lon: 32 (over y_lo, z, x).
Axes of the slice: x: 4, y: 4 (y_hi: 2, y_lo: 2; y = y_hi * 2 + y_lo), z: 4, core: 2. Of those that a mesh axis runs over, the one named last changes fastest.
Arguments:
- observations: bfloat16 [16384, 32, 256], P(('lat', 'lon')), may hold values from -6 to 6
- slot_cells: int32 [16384, 32], P(('lat', 'lon')), may hold values from 0 to 4095
- slot_counts: int32 [16384], P(('lat', 'lon')), may hold values from 4 to 32, as said below
- conv_in: bfloat16 [3, 3, 256, 512], replicated, may hold values from -0.125 to 0.125
- conv_density: float32 [3, 3, 512], replicated, may hold values from -3.5 to 3.5
- bias_in: float32 [512], replicated, may hold values from -3 to 3
- conv_mid: bfloat16 [3, 3, 512, 512], replicated, may hold values from -0.09375 to 0.09375
- bias_mid: float32 [512], replicated, may hold values from -3 to 3
Outputs:
- encoded: bfloat16 [32, 1024, 512], P('lat', 'lon')
Inputs may be any that keep to these rules, and one draw needn't show every extreme that they name: `slot_counts`: at most 32 live slots for each sender and tile pair; every tile receives 32 live rows from exactly one sender and fewer than 32 from each other sender.
All inputs are finite; a program needn't handle non-finite values.
Results may differ from a plain program's by a relative error of at most 0.0046.
Values may be sent and summed in bfloat16 or wider, within the bound.
A program may use at most 64 MiB of HBM per device.

v0:
```python
import math

import jax
import jax.numpy as jnp
from jax import lax
from jax.sharding import PartitionSpec as P

TH = 32
TW = 128


def shifted(array, axis, by):
    size = lax.axis_size(axis)
    return lax.ppermute(array, axis, [(i, (i + by) % size) for i in range(size)])


def passed_along(value, axis, steps):
    count = lax.axis_size(axis)
    leading, last = (max(0, -steps), min(count, count - steps))
    return lax.ppermute(value, axis, [(source, source + steps) for source in range(leading, last)])


def strided(padded, weight, rows, cols):
    total = jnp.zeros((rows * cols, weight.shape[-1]), jnp.float32)
    for a in range(3):
        for b in range(3):
            tap = padded[a : a + 2 * rows - 1 : 2, b : b + 2 * cols - 1 : 2]
            total = total + jnp.dot(
                tap.reshape(rows * cols, -1), weight[a, b], preferred_element_type=jnp.float32
            )
    return total.reshape(rows, cols, -1)


def density_term(padded, weight, rows, cols):
    total = jnp.zeros((rows, cols, weight.shape[-1]), jnp.float32)
    for a in range(3):
        for b in range(3):
            tap = padded[a : a + 2 * rows - 1 : 2, b : b + 2 * cols - 1 : 2].astype(jnp.float32)
            total = total + tap[:, :, None] * weight[a, b][None, None, :]
    return total


def layer_one(padded_mean, padded_fraction, conv_in, conv_density, bias_in, rows, cols):
    first = strided(padded_mean, conv_in, rows, cols) + density_term(
        padded_fraction, conv_density, rows, cols
    )
    return jax.nn.gelu(first + bias_in[None, None, :]).astype(jnp.bfloat16)


def on_device(
    observations, slot_cells, slot_counts, conv_in, conv_density, bias_in, conv_mid, bias_mid
):
    n_lat = lax.axis_size("lat")
    n_lon = lax.axis_size("lon")
    tiles = n_lat * n_lon
    slots = observations.shape[1]
    chans = observations.shape[2]
    cells = TH * TW
    recv_cells, recv_counts = (
        lax.all_to_all(slot_cells, ("lat", "lon"), split_axis=0, concat_axis=0, tiled=True),
        lax.all_to_all(slot_counts, ("lat", "lon"), split_axis=0, concat_axis=0, tiled=True),
    )
    received = lax.all_to_all(
        observations, ("lat", "lon"), split_axis=0, concat_axis=0, tiled=True
    ).reshape(tiles * slots, chans)
    live = jnp.arange(slots, dtype=jnp.int32)[None, :] < recv_counts[:, None]
    targets = jnp.where(live, recv_cells, -1).reshape(tiles * slots)
    total_rows = tiles * slots
    block = math.gcd(total_rows, 512)
    cell_ids = jnp.arange(cells, dtype=jnp.int32)

    def accumulate(step, carry):
        sums, density = carry
        start = step * block
        block_cells = lax.dynamic_slice_in_dim(targets, start, block, 0)
        block_rows = lax.dynamic_slice_in_dim(received, start, block, 0)
        onehot = (cell_ids[:, None] == block_cells[None, :]).astype(jnp.bfloat16)
        sums = sums + jnp.dot(onehot, block_rows, preferred_element_type=jnp.float32)
        density = density + jnp.sum(onehot, axis=1, dtype=jnp.float32)
        return (sums, density)

    start_sums = jnp.zeros((cells, chans), jnp.float32)
    start_density = jnp.zeros((cells,), jnp.float32)
    sums, density = lax.fori_loop(0, total_rows // block, accumulate, (start_sums, start_density))
    mean = (sums / jnp.maximum(density, 1.0)[:, None]).astype(jnp.bfloat16).reshape(TH, TW, chans)
    fraction = (density / (1.0 + density)).astype(jnp.bfloat16).reshape(TH, TW)
    edge = shifted((mean[:, -1:], fraction[:, -1:]), "lon", 1)
    wide_mean = jnp.concatenate([edge[0], mean], axis=1)
    wide_fraction = jnp.concatenate([edge[1], fraction], axis=1)
    upper = passed_along((wide_mean[-1:], wide_fraction[-1:]), "lat", 1)
    full_mean = jnp.concatenate([upper[0], wide_mean], axis=0)
    full_fraction = jnp.concatenate([upper[1], wide_fraction], axis=0)
    hidden = layer_one(full_mean, full_fraction, conv_in, conv_density, bias_in, TH // 2, TW // 2)
    side = shifted(hidden[:, -1:], "lon", 1)
    wide_hidden = jnp.concatenate([side, hidden], axis=1)
    top = passed_along(wide_hidden[-1:], "lat", 1)
    padded_hidden = jnp.concatenate([top, wide_hidden], axis=0)
    second = strided(padded_hidden, conv_mid, TH // 4, TW // 4)
    return jax.nn.gelu(second + bias_mid[None, None, :]).astype(jnp.bfloat16)


def solution(mesh):
    return jax.shard_map(
        on_device,
        mesh=mesh,
        in_specs=(
            P(("lat", "lon"), None, None),
            P(("lat", "lon"), None),
            P(("lat", "lon")),
            P(),
            P(),
            P(),
            P(),
            P(),
        ),
        out_specs=P("lat", "lon", None),
        check_vma=False,
    )
```

profile of v0, /device:TPU:1, one launch (start us, length us, event | category | flops | bytes accessed | tf_op | source)
XLA Modules:
  0.0 267.5 jit_solution(159686313888872376)
XLA Ops:
  0.0 1.4 copy.14
  1.4 11.5 %all-to-all-start = ((s32[128,1,1]{2,1,0:T(1,128)}), s32[128,1,1]{2,1,0:T(1,128)S(1)}, u32[]{:S(2)}, u32[]{:S(2)}) async-start(s32[128,1,1]{2,1,0:T(1,128)} %copy.14), calls=%async_computation | async-start | bytes 131072 | tf_op jit(solution)/shard_map/all_to_all | solution.py:61
  13.7 8.7 %all-to-all-done = s32[128,1,1]{2,1,0:T(1,128)S(1)} async-done(((s32[128,1,1]{2,1,0:T(1,128)}), s32[128,1,1]{2,1,0:T(1,128)S(1)}, u32[]{:S(2)}, u32[]{:S(2)}) %all-to-all-start) | async-done | bytes 544 | tf_op jit(solution)/shard_map/all_to_all | solution.py:61
  22.4 13.4 %all_to_all.26 = s32[128,1,32]{2,1,0:T(1,128)S(1)} all-to-all(s32[128,1,32]{2,1,0:T(1,128)S(1)} %bitcast.136), channel_id=1, replica_groups=mesh['lat'=4,'lon'=32] {'lat','lon'}, dimensions={0} | all-to-all | bytes 32768 | tf_op jit(solution)/shard_map/all_to_all | solution.py:60
  35.8 4.6 %all-to-all-start.2 = ((bf16[128,32,256]{2,1,0:T(8,128)(2,1)}), bf16[128,32,256]{2,1,0:T(8,128)(2,1)S(1)}, u32[]{:S(2)}, u32[]{:S(2)}) async-start(bf16[128,32,256]{2,1,0:T(8,128)(2,1)} %param.10), calls=%async_computation.2 | async-start | bytes 4194304 | tf_op jit(solution)/shard_map/all_to_all | solution.py:63
  40.4 2.4 reduce
  44.4 25.5 %all-to-all-done.2 = bf16[128,32,256]{2,1,0:T(8,128)(2,1)S(1)} async-done(((bf16[128,32,256]{2,1,0:T(8,128)(2,1)}), bf16[128,32,256]{2,1,0:T(8,128)(2,1)S(1)}, u32[]{:S(2)}, u32[]{:S(2)}) %all-to-all-start.2) | async-done | bytes 2097184 | tf_op jit(solution)/shard_map/all_to_all | solution.py:63
  69.9 54.0 %while.16 = (s32[]{:T(128)}, f32[4096,256]{1,0:T(8,128)}, f32[4096]{0:T(1024)S(1)}, s32[4096]{0:T(1024)S(1)}, bf16[4096,256]{1,0:T(8,128)(2,1)S(1)}, /*index=5*/s32[]{:T(128)}, s32[]{:T(128)}, s32[]{:T(128)}, s32[]{:T(128)}) while((s32[]{:T(128)}, f32[4096,256]{1,0:T(8,128)}, f32[4096]{0:T(1024)S(1)}, s32[4096]{0:T(1024)S(1)}, ...), condition=%wide.region_2.3_spmd.clone, body=%wide.region_0.2_spmd.clone.sunk | while | flops 1086328832 | bytes 8724638 | solution.py:84
  70.0 3.8 %fusion.104 = f32[4096,256]{1,0:T(8,128)} fusion(f32[4096,256]{1,0:T(8,128)} %get-tuple-element.199, s32[512]{0:T(512)S(1)} %dynamic_slice.21, pred[]{:T(512)S(6)} %compare.3, bf16[4096,256]{1,0:T(8,128)(2,1)S(1)} %get-tuple-element.211, s32[]{:T(128)S(6)} %select_n.17), kind=kOutput, calls=%fused_computation.5.clone.1 | convolution fusion | flops 1077936128 | bytes 8652805 | tf_op jit(solution)/shard_map/while/body/eval_jaxpr/dot_general | solution.py:78
  73.7 1.0 convert_reduce_fusion.2
  74.8 5.9 %fusion.104 = f32[4096,256]{1,0:T(8,128)} fusion(f32[4096,256]{1,0:T(8,128)} %get-tuple-element.199, s32[512]{0:T(512)S(1)} %dynamic_slice.21, pred[]{:T(512)S(6)} %compare.3, bf16[4096,256]{1,0:T(8,128)(2,1)S(1)} %get-tuple-element.211, s32[]{:T(128)S(6)} %select_n.17), kind=kOutput, calls=%fused_computation.5.clone.1 | convolution fusion | flops 1077936128 | bytes 8652805 | tf_op jit(solution)/shard_map/while/body/eval_jaxpr/dot_general | solution.py:78
  80.8 1.0 convert_reduce_fusion.2
  81.8 5.9 %fusion.104 = f32[4096,256]{1,0:T(8,128)} fusion(f32[4096,256]{1,0:T(8,128)} %get-tuple-element.199, s32[512]{0:T(512)S(1)} %dynamic_slice.21, pred[]{:T(512)S(6)} %compare.3, bf16[4096,256]{1,0:T(8,128)(2,1)S(1)} %get-tuple-element.211, s32[]{:T(128)S(6)} %select_n.17), kind=kOutput, calls=%fused_computation.5.clone.1 | convolution fusion | flops 1077936128 | bytes 8652805 | tf_op jit(solution)/shard_map/while/body/eval_jaxpr/dot_general | solution.py:78
  87.8 1.0 convert_reduce_fusion.2
  88.9 5.9 %fusion.104 = f32[4096,256]{1,0:T(8,128)} fusion(f32[4096,256]{1,0:T(8,128)} %get-tuple-element.199, s32[512]{0:T(512)S(1)} %dynamic_slice.21, pred[]{:T(512)S(6)} %compare.3, bf16[4096,256]{1,0:T(8,128)(2,1)S(1)} %get-tuple-element.211, s32[]{:T(128)S(6)} %select_n.17), kind=kOutput, calls=%fused_computation.5.clone.1 | convolution fusion | flops 1077936128 | bytes 8652805 | tf_op jit(solution)/shard_map/while/body/eval_jaxpr/dot_general | solution.py:78
  95.9 5.9 %fusion.104 = f32[4096,256]{1,0:T(8,128)} fusion(f32[4096,256]{1,0:T(8,128)} %get-tuple-element.199, s32[512]{0:T(512)S(1)} %dynamic_slice.21, pred[]{:T(512)S(6)} %compare.3, bf16[4096,256]{1,0:T(8,128)(2,1)S(1)} %get-tuple-element.211, s32[]{:T(128)S(6)} %select_n.17), kind=kOutput, calls=%fused_computation.5.clone.1 | convolution fusion | flops 1077936128 | bytes 8652805 | tf_op jit(solution)/shard_map/while/body/eval_jaxpr/dot_general | solution.py:78
  101.8 1.0 convert_reduce_fusion.2
  102.9 5.9 %fusion.104 = f32[4096,256]{1,0:T(8,128)} fusion(f32[4096,256]{1,0:T(8,128)} %get-tuple-element.199, s32[512]{0:T(512)S(1)} %dynamic_slice.21, pred[]{:T(512)S(6)} %compare.3, bf16[4096,256]{1,0:T(8,128)(2,1)S(1)} %get-tuple-element.211, s32[]{:T(128)S(6)} %select_n.17), kind=kOutput, calls=%fused_computation.5.clone.1 | convolution fusion | flops 1077936128 | bytes 8652805 | tf_op jit(solution)/shard_map/while/body/eval_jaxpr/dot_general | solution.py:78
  108.9 1.0 convert_reduce_fusion.2
  109.9 5.9 %fusion.104 = f32[4096,256]{1,0:T(8,128)} fusion(f32[4096,256]{1,0:T(8,128)} %get-tuple-element.199, s32[512]{0:T(512)S(1)} %dynamic_slice.21, pred[]{:T(512)S(6)} %compare.3, bf16[4096,256]{1,0:T(8,128)(2,1)S(1)} %get-tuple-element.211, s32[]{:T(128)S(6)} %select_n.17), kind=kOutput, calls=%fused_computation.5.clone.1 | convolution fusion | flops 1077936128 | bytes 8652805 | tf_op jit(solution)/shard_map/while/body/eval_jaxpr/dot_general | solution.py:78
  115.9 1.0 convert_reduce_fusion.2
  117.0 5.9 %fusion.104 = f32[4096,256]{1,0:T(8,128)} fusion(f32[4096,256]{1,0:T(8,128)} %get-tuple-element.199, s32[512]{0:T(512)S(1)} %dynamic_slice.21, pred[]{:T(512)S(6)} %compare.3, bf16[4096,256]{1,0:T(8,128)(2,1)S(1)} %get-tuple-element.211, s32[]{:T(128)S(6)} %select_n.17), kind=kOutput, calls=%fused_computation.5.clone.1 | convolution fusion | flops 1077936128 | bytes 8652805 | tf_op jit(solution)/shard_map/while/body/eval_jaxpr/dot_general | solution.py:78
  122.9 1.0 convert_reduce_fusion.2
  123.9 2.6 divide_convert_fusion
  126.6 5.3 %slice.198 = bf16[16,64,256]{2,1,0:T(8,128)(2,1)} slice(bf16[32,128,256]{2,1,0:T(8,128)(2,1)S(1)} %bitcast.108), slice={[1:32:2], [1:128:2], [0:256:1]} | slice | bytes 1048576 | tf_op jit(solution)/shard_map/slice | solution.py:27
  131.9 5.3 %slice.196 = bf16[16,64,256]{2,1,0:T(8,128)(2,1)} slice(bf16[32,128,256]{2,1,0:T(8,128)(2,1)S(1)} %bitcast.109), slice={[1:32:2], [0:127:2], [0:256:1]} | slice | bytes 1048576 | tf_op jit(solution)/shard_map/slice | solution.py:27
  140.0 2.9 %fusion.51 = f32[1024,512]{1,0:T(8,128)} fusion(bf16[1024,256]{1,0:T(8,128)(2,1)} %bitcast.122, bf16[3,3,256,512]{3,2,1,0:T(8,128)(2,1)} %param.13), kind=kOutput, calls=%fused_computation.69 | convolution fusion | flops 268435456 | bytes 2883584 | tf_op jit(solution)/shard_map/dot_general | solution.py:28
  142.8 2.8 %fusion.53 = f32[1024,512]{1,0:T(8,128)} fusion(bf16[1024,256]{1,0:T(8,128)(2,1)S(1)} %bitcast.121, bf16[3,3,256,512]{3,2,1,0:T(8,128)(2,1)} %param.13), kind=kOutput, calls=%fused_computation.71 | convolution fusion | flops 268435456 | bytes 2883584 | tf_op jit(solution)/shard_map/dot_general | solution.py:28
  145.6 2.8 %fusion.56 = f32[1024,512]{1,0:T(8,128)} fusion(bf16[1024,256]{1,0:T(8,128)(2,1)S(1)} %bitcast.120, bf16[3,3,256,512]{3,2,1,0:T(8,128)(2,1)} %param.13), kind=kOutput, calls=%fused_computation.74 | convolution fusion | flops 268435456 | bytes 2883584 | tf_op jit(solution)/shard_map/dot_general | solution.py:28
  148.4 2.7 %fusion.58 = f32[1024,512]{1,0:T(8,128)} fusion(bf16[1024,256]{1,0:T(8,128)(2,1)S(1)} %bitcast.119, bf16[3,3,256,512]{3,2,1,0:T(8,128)(2,1)} %param.13), kind=kOutput, calls=%fused_computation.76 | convolution fusion | flops 268435456 | bytes 2883584 | tf_op jit(solution)/shard_map/dot_general | solution.py:28
  151.1 1.2 collective-permute-start.2
  152.3 5.5 %collective-permute-done.2 = bf16[32,1]{1,0:T(8,128)(2,1)S(1)} collective-permute-done((bf16[32,1]{1,0:T(8,128)(2,1)S(1)}, bf16[32,1]{1,0:T(8,128)(2,1)S(1)}, u32[]{:S(2)}, u32[]{:S(2)}) %collective-permute-start.2) | collective-permute-done | bytes 96 | tf_op jit(solution)/shard_map/ppermute | solution.py:14
  157.9 5.5 %collective-permute-start.3 = (bf16[1,129]{1,0:T(2,128)(2,1)S(1)}, bf16[1,129]{1,0:T(2,128)(2,1)S(1)}, u32[]{:S(2)}, u32[]{:S(2)}) collective-permute-start(bf16[1,129]{1,0:T(2,128)(2,1)S(1)} %fusion.81), channel_id=1, source_target_pairs={{0,32},{32,64},{64,96},{1,33},{33,65},{65,97},{2,34},{34,66},{66,9... | collective-permute-start | bytes 782 | tf_op jit(solution)/shard_map/ppermute | solution.py:20
  164.8 5.9 %collective-permute-start.1 = (bf16[1,129,256]{2,1,0:T(8,128)(2,1)S(1)}, bf16[1,129,256]{2,1,0:T(8,128)(2,1)S(1)}, u32[]{:S(2)}, u32[]{:S(2)}) collective-permute-start(bf16[1,129,256]{2,1,0:T(8,128)(2,1)S(1)} %fusion.78), channel_id=1, source_target_pairs={{0,32},{32,64},{64,96},{1,33},{33,65},{65,97},{2,34},{34,66},{66,9... | collective-permute-start | bytes 198152 | tf_op jit(solution)/shard_map/ppermute | solution.py:20
  170.6 2.5 pad_maximum_fusion
  173.2 7.7 %slice.188 = bf16[16,64,256]{2,1,0:T(8,128)(2,1)S(1)} slice(bf16[32,129,256]{2,1,0:T(8,128)(2,1)} %pad_maximum_fusion), slice={[0:31:2], [0:127:2], [0:256:1]} | slice | bytes 1048576 | tf_op jit(solution)/shard_map/slice | solution.py:27
  180.9 2.7 %fusion.60 = f32[1024,512]{1,0:T(8,128)} fusion(bf16[1024,256]{1,0:T(8,128)(2,1)S(1)} %bitcast.126, bf16[3,3,256,512]{3,2,1,0:T(8,128)(2,1)} %param.13), kind=kOutput, calls=%fused_computation.78 | convolution fusion | flops 268435456 | bytes 2883584 | tf_op jit(solution)/shard_map/dot_general | solution.py:28
  183.6 7.7 %slice.194 = bf16[16,64,256]{2,1,0:T(8,128)(2,1)S(1)} slice(bf16[32,129,256]{2,1,0:T(8,128)(2,1)} %pad_maximum_fusion), slice={[1:32:2], [0:127:2], [0:256:1]} | slice | bytes 1048576 | tf_op jit(solution)/shard_map/slice | solution.py:27
  191.3 2.8 %maximum_maximum_fusion = bf16[33,129,256]{2,1,0:T(8,128)(2,1)} fusion(bf16[32,128,256]{2,1,0:T(8,128)(2,1)S(1)} %bitcast.114, bf16[32,1,256]{2,1,0:T(2,128)(2,1)S(1)} %collective-permute-done, bf16[1,129,256]{2,1,0:T(8,128)(2,1)S(1)} %collective-permute-done.1), kind=kLoop, calls=%fused_computation.14 | loop fusion | flops 6538752 | bytes 4359168 | tf_op jit(solution)/shard_map/concatenate | solution.py:91
  194.1 9.4 %slice.186 = bf16[16,64,256]{2,1,0:T(8,128)(2,1)} slice(bf16[33,129,256]{2,1,0:T(8,128)(2,1)} %maximum_maximum_fusion), slice={[0:31:2], [2:129:2], [0:256:1]} | slice | bytes 1048576 | tf_op jit(solution)/shard_map/slice | solution.py:27
  203.5 9.4 %slice.184 = bf16[16,64,256]{2,1,0:T(8,128)(2,1)} slice(bf16[33,129,256]{2,1,0:T(8,128)(2,1)} %maximum_maximum_fusion), slice={[0:31:2], [1:128:2], [0:256:1]} | slice | bytes 1048576 | tf_op jit(solution)/shard_map/slice | solution.py:27
  212.9 7.7 %slice.182 = bf16[16,64,256]{2,1,0:T(8,128)(2,1)S(1)} slice(bf16[33,129,256]{2,1,0:T(8,128)(2,1)} %maximum_maximum_fusion), slice={[0:31:2], [0:127:2], [0:256:1]} | slice | bytes 1048576 | tf_op jit(solution)/shard_map/slice | solution.py:27
  220.6 1.7 fusion.62
  222.3 1.7 fusion.64
  224.0 1.5 fusion.66
  225.8 2.0 add_add_fusion
  227.8 2.5 fusion.15
  231.4 1.3 fusion.33
  232.8 1.3 fusion.29
  234.1 2.7 %slice.232 = bf16[8,32,512]{2,1,0:T(8,128)(2,1)} slice(bf16[16,64,512]{2,1,0:T(8,128)(2,1)S(1)} %fusion.15), slice={[0:15:2], [1:64:2], [0:512:1]} | slice | bytes 524288 | tf_op jit(solution)/shard_map/slice | solution.py:27
  236.8 2.7 %slice.238 = bf16[8,32,512]{2,1,0:T(8,128)(2,1)} slice(bf16[16,64,512]{2,1,0:T(8,128)(2,1)S(1)} %fusion.15), slice={[1:16:2], [1:64:2], [0:512:1]} | slice | bytes 524288 | tf_op jit(solution)/shard_map/slice | solution.py:27
  239.5 1.9 collective-permute-start.5
  241.9 2.7 %slice.228 = bf16[8,32,512]{2,1,0:T(8,128)(2,1)} slice(bf16[16,65,512]{2,1,0:T(8,128)(2,1)S(1)} %pad_maximum_fusion.1), slice={[0:15:2], [0:63:2], [0:512:1]} | slice | bytes 524288 | tf_op jit(solution)/shard_map/slice | solution.py:27
  244.6 2.2 fusion.35
  246.8 2.7 %slice.234 = bf16[8,32,512]{2,1,0:T(8,128)(2,1)} slice(bf16[16,65,512]{2,1,0:T(8,128)(2,1)S(1)} %pad_maximum_fusion.1), slice={[1:16:2], [0:63:2], [0:512:1]} | slice | bytes 524288 | tf_op jit(solution)/shard_map/slice | solution.py:27
  250.0 2.8 %slice.226 = bf16[8,32,512]{2,1,0:T(8,128)(2,1)} slice(bf16[17,65,512]{2,1,0:T(8,128)(2,1)S(1)} %maximum_maximum_fusion.1), slice={[0:15:2], [2:65:2], [0:512:1]} | slice | bytes 524288 | tf_op jit(solution)/shard_map/slice | solution.py:27
  252.7 2.7 %slice.224 = bf16[8,32,512]{2,1,0:T(8,128)(2,1)} slice(bf16[17,65,512]{2,1,0:T(8,128)(2,1)S(1)} %maximum_maximum_fusion.1), slice={[0:15:2], [1:64:2], [0:512:1]} | slice | bytes 524288 | tf_op jit(solution)/shard_map/slice | solution.py:27
  255.4 2.7 %slice.222 = bf16[8,32,512]{2,1,0:T(8,128)(2,1)} slice(bf16[17,65,512]{2,1,0:T(8,128)(2,1)S(1)} %maximum_maximum_fusion.1), slice={[0:15:2], [0:63:2], [0:512:1]} | slice | bytes 524288 | tf_op jit(solution)/shard_map/slice | solution.py:27
  258.1 1.5 fusion.37
  259.6 1.5 fusion.39
  261.0 1.4 fusion.19
  262.5 1.4 convolution_add_fusion.2
  263.9 1.4 fusion.16
  265.3 1.3 convolution_add_fusion
  (96 shorter events, 11.2 us)
Async XLA Ops:
  1.4 21.0 %all-to-all-start = ((s32[128,1,1]{2,1,0:T(1,128)}), s32[128,1,1]{2,1,0:T(1,128)S(1)}, u32[]{:S(2)}, u32[]{:S(2)}) async-start(s32[128,1,1]{2,1,0:T(1,128)} %copy.14), calls=%async_computation | async-start | bytes 131072 | tf_op jit(solution)/shard_map/all_to_all | solution.py:61
  35.8 4.6 %copy-start.11 = (f32[3,3,512]{2,1,0:T(4,128)S(1)}, f32[3,3,512]{2,1,0:T(4,128)}, u32[]{:S(2)}) copy-start(f32[3,3,512]{2,1,0:T(4,128)} %param.14) | copy-start | bytes 55300
  35.8 34.1 %all-to-all-start.2 = ((bf16[128,32,256]{2,1,0:T(8,128)(2,1)}), bf16[128,32,256]{2,1,0:T(8,128)(2,1)S(1)}, u32[]{:S(2)}, u32[]{:S(2)}) async-start(bf16[128,32,256]{2,1,0:T(8,128)(2,1)} %param.10), calls=%async_computation.2 | async-start | bytes 4194304 | tf_op jit(solution)/shard_map/all_to_all | solution.py:63
  139.5 3.4 %copy-start.6 = (bf16[16,64,256]{2,1,0:T(8,128)(2,1)S(1)}, bf16[16,64,256]{2,1,0:T(8,128)(2,1)}, u32[]{:S(2)}) copy-start(bf16[16,64,256]{2,1,0:T(8,128)(2,1)} %slice.196) | copy-start | bytes 1572868
  139.5 25.3 %collective-permute-start = (bf16[32,1,256]{2,1,0:T(2,128)(2,1)S(1)}, bf16[32,1,256]{2,1,0:T(2,128)(2,1)S(1)}, u32[]{:S(2)}, u32[]{:S(2)}) collective-permute-start(bf16[32,1,256]{2,1,0:T(2,128)(2,1)S(1)} %slice.240), channel_id=1, source_target_pairs={{0,1},{1,2},{2,3},{3,4},{4,5},{5,6},{6,7},{7,8},{8,9},{9,10},{10,1... | collective-permute-start | bytes 49160 | tf_op jit(solution)/shard_map/ppermute | solution.py:14
  151.1 6.7 %collective-permute-start.2 = (bf16[32,1]{1,0:T(8,128)(2,1)S(1)}, bf16[32,1]{1,0:T(8,128)(2,1)S(1)}, u32[]{:S(2)}, u32[]{:S(2)}) collective-permute-start(bf16[32,1]{1,0:T(8,128)(2,1)S(1)} %slice.243), channel_id=1, source_target_pairs={{0,1},{1,2},{2,3},{3,4},{4,5},{5,6},{6,7},{7,8},{8,9},{9,10},{10,1... | collective-permute-start | bytes 200 | tf_op jit(solution)/shard_map/ppermute | solution.py:14
  157.9 6.2 %collective-permute-start.3 = (bf16[1,129]{1,0:T(2,128)(2,1)S(1)}, bf16[1,129]{1,0:T(2,128)(2,1)S(1)}, u32[]{:S(2)}, u32[]{:S(2)}) collective-permute-start(bf16[1,129]{1,0:T(2,128)(2,1)S(1)} %fusion.81), channel_id=1, source_target_pairs={{0,32},{32,64},{64,96},{1,33},{33,65},{65,97},{2,34},{34,66},{66,9... | collective-permute-start | bytes 782 | tf_op jit(solution)/shard_map/ppermute | solution.py:20
  164.8 26.5 %collective-permute-start.1 = (bf16[1,129,256]{2,1,0:T(8,128)(2,1)S(1)}, bf16[1,129,256]{2,1,0:T(8,128)(2,1)S(1)}, u32[]{:S(2)}, u32[]{:S(2)}) collective-permute-start(bf16[1,129,256]{2,1,0:T(8,128)(2,1)S(1)} %fusion.78), channel_id=1, source_target_pairs={{0,32},{32,64},{64,96},{1,33},{33,65},{65,97},{2,34},{34,66},{66,9... | collective-permute-start | bytes 198152 | tf_op jit(solution)/shard_map/ppermute | solution.py:20
  203.5 22.1 %copy-start.4 = (f32[1024,512]{1,0:T(8,128)S(1)}, f32[1024,512]{1,0:T(8,128)}, u32[]{:S(2)}) copy-start(f32[1024,512]{1,0:T(8,128)} %fusion.60) | copy-start | bytes 6291460
  220.6 5.0 %copy-start.2 = (f32[1024,512]{1,0:T(8,128)S(1)}, f32[1024,512]{1,0:T(8,128)}, u32[]{:S(2)}) copy-start(f32[1024,512]{1,0:T(8,128)} %fusion.56) | copy-start | bytes 6291460
  220.6 5.0 %copy-start.3 = (f32[1024,512]{1,0:T(8,128)S(1)}, f32[1024,512]{1,0:T(8,128)}, u32[]{:S(2)}) copy-start(f32[1024,512]{1,0:T(8,128)} %fusion.58) | copy-start | bytes 6291460
  222.3 3.3 %copy-start.1 = (f32[1024,512]{1,0:T(8,128)S(1)}, f32[1024,512]{1,0:T(8,128)}, u32[]{:S(2)}) copy-start(f32[1024,512]{1,0:T(8,128)} %fusion.53) | copy-start | bytes 6291460
  224.0 1.8 copy-start
  225.8 2.0 copy-start.12
  231.3 8.2 %collective-permute-start.4 = (bf16[16,1,512]{2,1,0:T(2,128)(2,1)S(1)}, bf16[16,1,512]{2,1,0:T(2,128)(2,1)S(1)}, u32[]{:S(2)}, u32[]{:S(2)}) collective-permute-start(bf16[16,1,512]{2,1,0:T(2,128)(2,1)S(1)} %slice.246), channel_id=1, source_target_pairs={{0,1},{1,2},{2,3},{3,4},{4,5},{5,6},{6,7},{7,8},{8,9},{9,10},{10,1... | collective-permute-start | bytes 49160 | tf_op jit(solution)/shard_map/ppermute | solution.py:14
  239.5 10.0 %collective-permute-start.5 = (bf16[1,65,512]{2,1,0:T(8,128)(2,1)S(1)}, bf16[1,65,512]{2,1,0:T(8,128)(2,1)S(1)}, u32[]{:S(2)}, u32[]{:S(2)}) collective-permute-start(bf16[1,65,512]{2,1,0:T(8,128)(2,1)S(1)} %fusion.77), channel_id=1, source_target_pairs={{0,32},{32,64},{64,96},{1,33},{33,65},{65,97},{2,34},{34,66},{66,9... | collective-permute-start | bytes 199688 | tf_op jit(solution)/shard_map/ppermute | solution.py:20
  250.0 11.1 %copy-start.5 = (f32[256,512]{1,0:T(8,128)S(1)}, f32[256,512]{1,0:T(8,128)}, u32[]{:S(2)}) copy-start(f32[256,512]{1,0:T(8,128)} %fusion.35) | copy-start | bytes 1572868
  258.1 3.0 %copy-start.10 = (bf16[8,32,512]{2,1,0:T(8,128)(2,1)S(1)}, bf16[8,32,512]{2,1,0:T(8,128)(2,1)}, u32[]{:S(2)}) copy-start(bf16[8,32,512]{2,1,0:T(8,128)(2,1)} %slice.222) | copy-start | bytes 786436
  259.5 2.9 %copy-start.8 = (bf16[8,32,512]{2,1,0:T(8,128)(2,1)S(1)}, bf16[8,32,512]{2,1,0:T(8,128)(2,1)}, u32[]{:S(2)}) copy-start(bf16[8,32,512]{2,1,0:T(8,128)(2,1)} %slice.232) | copy-start | bytes 786436
  261.0 2.9 %copy-start.9 = (bf16[8,32,512]{2,1,0:T(8,128)(2,1)S(1)}, bf16[8,32,512]{2,1,0:T(8,128)(2,1)}, u32[]{:S(2)}) copy-start(bf16[8,32,512]{2,1,0:T(8,128)(2,1)} %slice.234) | copy-start | bytes 786436
  262.5 2.8 %copy-start.7 = (bf16[8,32,512]{2,1,0:T(8,128)(2,1)S(1)}, bf16[8,32,512]{2,1,0:T(8,128)(2,1)}, u32[]{:S(2)}) copy-start(bf16[8,32,512]{2,1,0:T(8,128)(2,1)} %slice.238) | copy-start | bytes 786436
  263.9 2.7 %copy-start.13 = (f32[512]{0:T(512)S(1)}, f32[512]{0:T(512)}, u32[]{:S(2)}) copy-start(f32[512]{0:T(512)} %param.17) | copy-start | bytes 6148
where the time goes:
time: 270 us; the launch traced here: 268 us
  matrix products  79.5 us (29%)
  local copies, waits for them, and re-layouts  79.2 us (29%)
  waiting for transfers between devices  40 us (15%)
  starting transfers between devices  31.2 us (12%)
  other arithmetic  23.4 us (9%)
  blocking collectives  13.4 us (5%)
    slice x18, local copies, waits for them, and re-layouts, strided(): tap = padded[a:a + 2 * rows - 1:2, b:b + 2 * cols - 1:2]  73.9 us
    dot_general x8, matrix products, accumulate(): jnp.dot(onehot, block_rows, preferred_element_type=jnp.float32)  45.4 us
    dot_general x18, matrix products, strided(): jnp.dot(tap.reshape(rows * cols, -1), weight[a, b], preferred_element_typ...  34.1 us
    all_to_all x1, waiting for transfers between devices, on_device(): lax.all_to_all(observations, ('lat', 'lon'), split_axis=0, concat_axis=0,...  25.5 us
    all_to_all x1, blocking collectives, on_device(): lax.all_to_all(slot_cells, ('lat', 'lon'), split_axis=0, concat_axis=0, t...  13.4 us
    ppermute x3, starting transfers between devices, passed_along(): lax.ppermute(value, axis, [(source, source + steps) for source in range(l...  13.3 us
    all_to_all x1, starting transfers between devices, on_device(): lax.all_to_all(slot_counts, ('lat', 'lon'), split_axis=0, concat_axis=0,...  11.5 us
    all_to_all x1, waiting for transfers between devices, on_device(): lax.all_to_all(slot_counts, ('lat', 'lon'), split_axis=0, concat_axis=0,...  8.66 us
  transfers between devices with their start and end apart: 8, of which 4 were waited for; matrix products, arithmetic and copies ran while one was open for 20% of the time, Pallas kernels for 0%

commit v1 on v0

v1 whole, which is shorter than its diff:
```python
import functools

import jax
import jax.numpy as jnp
from jax import lax
from jax.experimental import pallas as pl
from jax.experimental.pallas import tpu as pltpu
from jax.sharding import PartitionSpec as P

MESH = pl.DeviceIdType.MESH
N = 128
SLOTS = 32
CH = 256
HID = 512
WIDE = CH + 128
GROUPS = 8
PER = N // GROUPS
K1 = 9 * CH
K2 = 9 * HID
F32 = jnp.float32
BF16 = jnp.bfloat16


def position():
    lat = lax.axis_index("lat")
    lon = lax.axis_index("lon")
    return lon & 3, ((lat >> 1) << 1) + (lon >> 4), (lon >> 2) & 3, lat & 1


def partner(here, bb, cc, aa, dc, sign):
    x, y, z, core = here
    x = (x + sign * aa) & 3
    y = (y + sign * (aa + bb)) & 3
    z = (z + sign * (aa + cc)) & 3
    core = core ^ dc
    return (y & 2) + core, ((y & 1) << 4) + (z << 2) + x


def gelu(x):
    return 0.5 * x * (1.0 + jnp.tanh(0.7978845608028654 * (x + 0.044715 * (x * x * x))))


def one_hot(ids, tag, want, height):
    if tag is not None:
        ids = jnp.where(tag == want, ids, jnp.full_like(ids, -1.0))
    rows = lax.broadcasted_iota(jnp.int32, (height, 128), 0).astype(F32).astype(BF16)
    rows = rows.reshape(height // 16, 16, 128)
    hit = rows == ids[None]
    return jnp.where(hit, jnp.ones_like(rows), jnp.zeros_like(rows)).reshape(height, 128)


def first_row(block, row):
    sub = lax.broadcasted_iota(jnp.int32, block.shape, 0)
    return jnp.where(sub == 0, jnp.broadcast_to(row, block.shape), block)


def down_one(block, row):
    return first_row(pltpu.roll(block, 1, 0), row)


def offset(q, ip, i):
    return ip * (576 if q else 512) + i * 64


def kernel(
    obs, cells, counts, w1, wd, b1, w2, b2, out,
    rows_in, meta_out, meta_in, acc, dens, edge, edge_bf, corner, corner_bf, top_in, left_in, corner_in,
    x0, x1, xe, hid0, hid1, ext, w1v, w2v, wdf,
    send, recv, msend, mrecv, wsem, hsend, hrecv,
):
    here = position()
    lat = lax.axis_index("lat")
    lon = lax.axis_index("lon")

    def each(fn):
        for i in range(8):
            fn(i, 0, 0, i >> 1, i & 1)

        def body(o, carry):
            for i in range(8):
                fn(o * 8 + i, o >> 2, o & 3, i >> 1, i & 1)
            return carry

        lax.fori_loop(1, 16, body, 0)

    barrier = pltpu.get_barrier_semaphore()

    def greet(k, bb, cc, aa, dc):
        if isinstance(k, int) and k == 0:
            return
        pl.semaphore_signal(
            barrier, inc=1, device_id=partner(here, bb, cc, aa, dc, -1), device_id_type=MESH
        )

    each(greet)
    w1_copy = pltpu.make_async_copy(w1, w1v.at[pl.ds(0, K1)], wsem.at[0])
    w2_copy = pltpu.make_async_copy(w2, w2v, wsem.at[1])
    w1_copy.start()
    w2_copy.start()

    lane = lax.broadcasted_iota(jnp.int32, (N, 128), 1)
    sub = lax.broadcasted_iota(jnp.int32, (N, 128), 0)
    column = jnp.sum(
        jnp.where(lane == sub, jnp.broadcast_to(counts[...], (N, 128)), 0), axis=1, keepdims=True
    )
    cell_block = cells[...]
    wide_cells = jnp.concatenate([cell_block] * 4, axis=1)
    coded = jnp.where((lane & 31) < column, wide_cells, -1)
    for v in range(4):
        meta_out[v] = jnp.where((lane >> 5) == v, coded, 0).reshape(N, 1, 128)
    acc[...] = jnp.zeros_like(acc)
    dens[...] = jnp.zeros_like(dens)
    edge[...] = jnp.zeros_like(edge)
    wdf[...] = jnp.zeros_like(wdf)
    wdf[0:9, :] = wd[...]
    taps = wdf[...]
    taps_hi = taps.astype(BF16)
    taps_lo = (taps - taps_hi.astype(F32)).astype(BF16)
    w1v[pl.ds(K1, 128), :] = jnp.concatenate(
        [taps_hi, taps_lo, jnp.zeros((96, HID), BF16)], axis=0
    )

    pl.semaphore_wait(barrier, N - 1)

    def dispatch(k, bb, cc, aa, dc):
        to_lat, to_lon = partner(here, bb, cc, aa, dc, 1)
        to = to_lat * 32 + to_lon
        v = (aa * 2 + dc) & 3
        if isinstance(k, int) and k == 0:
            pltpu.make_async_copy(meta_out.at[v, pl.ds(to, 1)], meta_in.at[pl.ds(0, 1)], mrecv.at[0]).start()
            pltpu.make_async_copy(obs.at[pl.ds(to, 1)], rows_in.at[pl.ds(0, 1)], recv.at[0]).start()
            return
        pltpu.make_async_remote_copy(
            src_ref=meta_out.at[v, pl.ds(to, 1)], dst_ref=meta_in.at[pl.ds(k, 1)],
            send_sem=msend, recv_sem=mrecv.at[k // PER],
            device_id=(to_lat, to_lon), device_id_type=MESH,
        ).start()
        pltpu.make_async_remote_copy(
            src_ref=obs.at[pl.ds(to, 1)], dst_ref=rows_in.at[pl.ds(k, 1)],
            send_sem=send, recv_sem=recv.at[k // PER],
            device_id=(to_lat, to_lon), device_id_type=MESH,
        ).start()

    each(dispatch)

    def spread(v):
        return jnp.broadcast_to(v.astype(F32), (16, 128)).astype(BF16)

    def codes(g):
        result = []
        for t in range(4):
            cell = sum(meta_in[g * PER + 4 * t + u] for u in range(4))
            alive = cell >= 0
            r = cell >> 7
            c = cell & 127
            col = (c & 1) * 64 + ((c >> 1) & 1) * 32 + (c >> 2)
            row = (r & 1) * 16 + ((r >> 1) & 1) * 8 + (r >> 2)
            pos = (
                (r & 1) * 2048 + (c & 1) * 1024 + ((r >> 1) & 1) * 512 + (r >> 2) * 64
                + ((c >> 1) & 1) * 32 + (c >> 2)
            )
            result.append(
                (
                    spread(pos & 255),
                    spread(jnp.where(alive, pos >> 8, 99)),
                    spread(pos & 127),
                    spread(jnp.where(alive, pos >> 7, 199)),
                    spread(col),
                    spread(jnp.where(alive, r - 29, 99)),
                    spread(jnp.where(alive & (c >= 125), (c - 125) * 32 + row, -1)),
                )
            )
        return result

    def gather_edges(code, block):
        wide = jnp.concatenate([block, jnp.ones((PER * SLOTS, 128), BF16)], axis=1)
        for e in range(4):
            if e < 3:
                hot = [one_hot(code[t][4], code[t][5], e, 128) for t in range(4)]
            else:
                hot = [one_hot(code[t][6], None, None, 128) for t in range(4)]
            at = pl.ds(e * 128, 128)
            edge[at, :] += jnp.dot(jnp.concatenate(hot, axis=1), wide, preferred_element_type=F32)

    def gather_cells(code, block):
        lows = jnp.concatenate([one_hot(code[t][2], None, None, 128) for t in range(4)], axis=1)
        highs = jnp.concatenate([one_hot(code[t][3], None, None, 128) for t in range(4)], axis=1)
        dens[...] += lax.dot_general(lows, highs, (((1,), (1,)), ((), ())), preferred_element_type=F32)
        for b in range(16):
            hot = jnp.concatenate([one_hot(code[t][0], code[t][1], b, 256) for t in range(4)], axis=1)
            at = pl.ds(b * 256, 256)
            acc[at, :] += jnp.dot(hot, block, preferred_element_type=F32)

    def arrived(g):
        pltpu.make_async_copy(
            meta_out.at[0, pl.ds(g * PER, PER)], meta_in.at[pl.ds(g * PER, PER)], mrecv.at[g]
        ).wait()
        pltpu.make_async_copy(
            obs.at[pl.ds(g * PER, PER)], rows_in.at[pl.ds(g * PER, PER)], recv.at[g]
        ).wait()
        return codes(g), rows_in[pl.ds(g * PER, PER)].reshape(PER * SLOTS, CH)

    def group(g, carry):
        code, block = arrived(g)
        gather_edges(code, block)
        gather_cells(code, block)
        return carry

    lax.fori_loop(0, GROUPS - 1, group, 0)
    code, block = arrived(GROUPS - 1)
    gather_edges(code, block)

    amount = edge[:, CH:]
    scale = 1.0 / jnp.maximum(amount, 1.0)
    edge[...] = jnp.concatenate(
        [edge[:, 0:128] * scale, edge[:, 128:CH] * scale, amount / (1.0 + amount)], axis=1
    )
    edge_bf[...] = edge[...].astype(BF16)
    corner[...] = jnp.zeros_like(corner)
    for a in range(3):
        for b, at in enumerate((95, 63, 127)):
            corner[pl.ds(a * 3 + b, 1), :] = edge[pl.ds(a * 128 + at, 1), :]
    corner_bf[...] = corner[...].astype(BF16)
    next_lat = (lat + 1) & 3
    next_lon = (lon + 1) & 31
    halos = [
        pltpu.make_async_remote_copy(
            src_ref=src, dst_ref=dst, send_sem=hsend.at[i], recv_sem=hrecv.at[i],
            device_id=to, device_id_type=MESH,
        )
        for i, (src, dst, to) in enumerate(
            (
                (edge_bf.at[pl.ds(0, 384)], top_in, (next_lat, lon)),
                (edge_bf.at[pl.ds(384, 96)], left_in, (lat, next_lon)),
                (corner_bf, corner_in, (next_lat, next_lon)),
            )
        )
    ]
    for halo in halos:
        halo.start()

    gather_cells(code, block)

    count = dens[...]
    scale_all = 1.0 / jnp.maximum(count, 1.0)
    fraction_all = count / (1.0 + count)
    for h in range(32):
        scale = jnp.broadcast_to(scale_all[:, h : h + 1], (128, 128))
        fraction = jnp.broadcast_to(fraction_all[:, h : h + 1], (128, 128))
        sums = acc[pl.ds(h * 128, 128), :]
        value = jnp.concatenate([sums[:, 0:128] * scale, sums[:, 128:CH] * scale, fraction], axis=1)
        q, p, ip, i = h >> 4, (h >> 3) & 1, (h >> 2) & 1, (h & 3) * 2
        x = x1 if q else x0
        x[p, pl.ds(offset(q, ip, i), 128), :] = value.astype(BF16)
        if p:
            for half in range(2):
                part = value[half * 64 : half * 64 + 64]
                moved = jnp.concatenate([pltpu.roll(part[32:64], 1, 0), part[0:32]], axis=0)
                x[2, pl.ds(offset(q, ip, i + half), 64), :] = moved.astype(BF16)

    for halo in halos:
        halo.wait()

    inside = jnp.where(lat > 0, 1.0, 0.0).astype(F32)
    left = left_in[...].astype(F32)
    diag = corner_in[...].astype(F32) * inside
    for a in range(3):
        p0 = top_in[pl.ds(a * 128, 64), :].astype(F32) * inside
        p1 = top_in[pl.ds(a * 128 + 64, 64), :].astype(F32) * inside
        moved = jnp.concatenate([down_one(p1[32:64], diag[a * 3 + 2 : a * 3 + 3]), p1[0:32]], axis=0)
        for b, top in enumerate((moved, p0, p1)):
            side = left[b * 32 : b * 32 + 32]
            if a == 0:
                side = jnp.concatenate([down_one(side[24:32], diag[6 + b : 7 + b]), side[16:24]], axis=0)
            else:
                side = side[(a - 1) * 16 : a * 16]
            angle = first_row(jnp.zeros((16, WIDE), F32), diag[a * 3 + b : a * 3 + b + 1])
            top = top.astype(BF16)
            xe[a * 3 + b, pl.ds(0, 64), :] = top
            xe[a * 3 + b, pl.ds(64, 16), :] = side.astype(BF16)
            xe[a * 3 + b, pl.ds(80, 16), :] = angle.astype(BF16)
            if a == 2:
                x1[(2, 0, 1)[b], pl.ds(512, 64), :] = top
    for q in range(2):
        x = x1 if q else x0
        for ip in range(2):
            for i in range(8):
                at = pl.ds(offset(q, ip, i), 16)
                t = 64 + q * 16 + ip * 8 + i
                x[2, at, :] = first_row(x[2, at, :].astype(F32), left[t : t + 1]).astype(BF16)

    w1_copy.wait()
    lanes = lax.broadcasted_iota(jnp.int32, (16, 128), 1)
    tap_of_lane = jnp.where(lanes < 32, lanes & 15, 99).astype(F32).astype(BF16)
    bias1 = b1[...]
    for chunk in range(4):
        ip, half = chunk >> 1, chunk & 1
        parts = []
        shares = None
        for a in range(3):
            for b in range(3):
                v = (2, 0, 1)[b]
                if a == 1:
                    x, at = x0, ip * 512 + half * 256
                elif a == 2:
                    x, at = x1, ip * 576 + half * 256
                else:
                    x, at = x1, (0 if ip else 512) + half * 256
                data = x[v, pl.ds(at, 256), :]
                if chunk == 0:
                    data = jnp.concatenate([xe[a * 3 + b], data], axis=0)
                parts.append(data[:, 0:CH])
                share = data[:, CH:].reshape(-1, 16, 128)
                if shares is None:
                    shares = jnp.zeros_like(share)
                shares = jnp.where((tap_of_lane == a * 3 + b)[None], share, shares)
        parts.append(shares.reshape(-1, 128))
        first = jnp.dot(jnp.concatenate(parts, axis=1), w1v[...], preferred_element_type=F32)
        hidden = gelu(first + bias1)
        if chunk == 0:
            ext[...] = hidden[0:96]
            hidden = hidden[96:]
            above0 = ext[pl.ds(0, 32), :] * inside
            above1 = ext[pl.ds(32, 32), :] * inside
            hid1[0, pl.ds(0, 32), :] = above0.astype(BF16)
            hid1[1, pl.ds(0, 32), :] = above1.astype(BF16)
            hid1[2, pl.ds(0, 32), :] = down_one(above1, ext[pl.ds(80, 1), :] * inside).astype(BF16)
        hid = hid1 if ip else hid0
        for k in range(4):
            i = half * 4 + k
            at = pl.ds(i * 32 + (32 if ip else 0), 32)
            even = hidden[k * 64 : k * 64 + 32]
            odd = hidden[k * 64 + 32 : k * 64 + 64]
            hid[0, at, :] = even.astype(BF16)
            hid[1, at, :] = odd.astype(BF16)
            hid[2, at, :] = down_one(odd, ext[pl.ds(64 + ip * 8 + i, 1), :]).astype(BF16)

    w2_copy.wait()
    parts = []
    for a in range(3):
        for b in range(3):
            v = (2, 0, 1)[b]
            if a == 1:
                parts.append(hid0[v])
            else:
                parts.append(hid1[v, pl.ds(32 if a == 2 else 0, 256), :])
    second = jnp.dot(jnp.concatenate(parts, axis=1), w2v[...], preferred_element_type=F32)
    out[...] = gelu(second + b2[...]).astype(BF16).reshape(8, 32, HID)

    pltpu.make_async_copy(obs.at[pl.ds(1, N - 1)], rows_in.at[pl.ds(1, N - 1)], send).wait()
    pltpu.make_async_copy(
        meta_out.at[0, pl.ds(1, N - 1)], meta_in.at[pl.ds(1, N - 1)], msend
    ).wait()


def on_device(obs, cells, counts, conv_in, conv_density, bias_in, conv_mid, bias_mid):
    vmem = pl.BlockSpec(memory_space=pltpu.VMEM)
    hbm = pl.BlockSpec(memory_space=pl.ANY)
    dma = pltpu.SemaphoreType.DMA
    return pl.pallas_call(
        kernel,
        out_shape=jax.ShapeDtypeStruct((8, 32, HID), BF16),
        in_specs=[hbm, vmem, vmem, hbm, vmem, vmem, hbm, vmem],
        out_specs=vmem,
        scratch_shapes=[
            pltpu.VMEM((N, SLOTS, CH), BF16),
            pltpu.VMEM((4, N, 1, 128), jnp.int32),
            pltpu.VMEM((N, 1, 128), jnp.int32),
            pltpu.VMEM((4096, CH), F32),
            pltpu.VMEM((128, 128), F32),
            pltpu.VMEM((512, WIDE), F32),
            pltpu.VMEM((512, WIDE), BF16),
            pltpu.VMEM((16, WIDE), F32),
            pltpu.VMEM((16, WIDE), BF16),
            pltpu.VMEM((384, WIDE), BF16),
            pltpu.VMEM((96, WIDE), BF16),
            pltpu.VMEM((16, WIDE), BF16),
            pltpu.VMEM((3, 1024, WIDE), BF16),
            pltpu.VMEM((3, 1088, WIDE), BF16),
            pltpu.VMEM((9, 96, WIDE), BF16),
            pltpu.VMEM((3, 256, HID), BF16),
            pltpu.VMEM((3, 288, HID), BF16),
            pltpu.VMEM((96, HID), F32),
            pltpu.VMEM((K1 + 128, HID), BF16),
            pltpu.VMEM((K2, HID), BF16),
            pltpu.VMEM((16, HID), F32),
            dma,
            dma((GROUPS,)),
            dma,
            dma((GROUPS,)),
            dma((2,)),
            dma((3,)),
            dma((3,)),
        ],
        compiler_params=pltpu.CompilerParams(
            collective_id=0, has_side_effects=True, vmem_limit_bytes=56 * 2**20
        ),
    )(
        obs,
        cells,
        counts.reshape(1, N),
        conv_in.reshape(K1, HID),
        conv_density.reshape(9, HID),
        bias_in.reshape(1, HID),
        conv_mid.reshape(K2, HID),
        bias_mid.reshape(1, HID),
    )


def solution(mesh):
    return jax.shard_map(
        on_device,
        mesh=mesh,
        in_specs=(
            P(("lat", "lon"), None, None),
            P(("lat", "lon"), None),
            P(("lat", "lon")),
            P(),
            P(),
            P(),
            P(),
            P(),
        ),
        out_specs=P("lat", "lon", None),
        check_vma=False,
    )
```

time: 270 us -> 58 us (0.21)
  matrix products: 79.5 us -> 0 us
  local copies, waits for them, and re-layouts: 79.2 us -> 4.46 us
  Pallas kernels: 0 us -> 52.3 us
  waiting for transfers between devices: 40 us -> 0 us
  starting transfers between devices: 31.2 us -> 0 us
  other arithmetic: 23.4 us -> 0 us
  blocking collectives: 13.4 us -> 0 us
    dot_general x26 -> x0, matrix products: 79.5 us -> none  [the longest x8 45.4 us: accumulate(): jnp.dot(onehot, block_rows, preferred_element_type=jnp.float32)]
    slice x31 -> x0, local copies, waits for them, and re-layouts: 75.5 us -> none  [the longest x18 73.9 us: strided(): tap = padded[a:a + 2 * rows - 1:2, b:b + 2 * cols - 1:2]]
    pallas_call x0 -> x1, Pallas kernels: none -> 52.3 us  [on_device(): pl.pallas_call(kernel, out_shape=jax.ShapeDtypeStruct((8, 32, HID), BF16)...]
    all_to_all x2 -> x0, waiting for transfers between devices: 34.2 us -> none  [the longest x1 25.5 us: on_device(): lax.all_to_all(observations, ('lat', 'lon'), split_axis=0, concat_axis=0,...]
    all_to_all x2 -> x0, starting transfers between devices: 16.1 us -> none  [the longest x1 11.5 us: on_device(): lax.all_to_all(slot_counts, ('lat', 'lon'), split_axis=0, concat_axis=0,...]
    ppermute x6 -> x0, starting transfers between devices: 15.1 us -> none  [the longest x3 13.3 us: passed_along(): lax.ppermute(value, axis, [(source, source + steps) for source in range(l...]
    all_to_all x1 -> x0, blocking collectives: 13.4 us -> none  [on_device(): lax.all_to_all(slot_cells, ('lat', 'lon'), split_axis=0, concat_axis=0, t...]
    reduce_sum x8 -> x0, other arithmetic: 7.7 us -> none  [accumulate(): density = density + jnp.sum(onehot, axis=1, dtype=jnp.float32)]
  transfers between devices with their start and end apart: 8 -> 0, of which waited for: 4 -> 0; matrix products, arithmetic and copies ran while one was open for 20% -> 0% of each run, Pallas kernels for 0% -> 0%
where the time goes in v1:
time: 58 us; the launch traced here: 56.8 us
  Pallas kernels  52.3 us (90%)
  local copies, waits for them, and re-layouts  4.46 us (8%)
    pallas_call x1, Pallas kernels, on_device(): pl.pallas_call(kernel, out_shape=jax.ShapeDtypeStruct((8, 32, HID), BF16)...  52.3 us
    unnamed x2, local copies, waits for them, and re-layouts  3.12 us
    reshape x1, local copies, waits for them, and re-layouts, on_device(): conv_density.reshape(9, HID)  1.35 us

profile of v1, /device:TPU:1, one launch (start us, length us, event | category | flops | bytes accessed | tf_op | source)
XLA Modules:
  0.0 56.8 jit_solution(10051264044942117227)
XLA Ops:
  0.0 1.3 %reshape.20.wd = f32[9,512]{1,0:T(8,128)} reshape(f32[3,3,512]{2,1,0:T(4,128)} %param.12) | data formatting | bytes 36864 | tf_op jit(solution)/shard_map/reshape | solution.py:403
  1.3 1.4 %copy.9.cells = s32[128,32]{1,0:T(8,128)} copy(s32[128,32]{0,1:T(8,128)} %param.9) | data formatting | bytes 32768 | tf_op args[1]
  2.8 52.3 %shard_map.82 = bf16[8,32,512]{2,1,0:T(8,128)(2,1)} custom-call(bf16[128,32,256]{2,1,0:T(8,128)(2,1)} %obs.1, s32[128,32]{1,0:T(8,128)} %copy.9.cells, s32[1,128]{1,0:T(1,128)} %bitcast.9, bf16[2304,512]{1,0:T(8,128)(2,1)} %bitcast.6, f32[9,512]{1,0:T(8,128)} %reshape.20.wd, f32[1,512]{1,0:T(1,128)} %bitcast.7, bf16[4608,512]{1,0:T(8,128)(2,1)} %bitcast.5, ...), custom_call_target="tpu_custom_call" | custom-call | tf_op jit(solution)/shard_map/pallas_call | solution.py:360
  55.1 1.7 %copy.11 = bf16[8,32,512]{2,1,0:T(8,128)(2,1)} copy(bf16[8,32,512]{2,1,0:T(8,128)(2,1)} %shard_map.82) | data formatting | bytes 524288

commit v2 on v1

--- a/solution.py
+++ b/solution.py
@@ -13,8 +13,8 @@
 CH = 256
 HID = 512
 WIDE = CH + 128
-GROUPS = 8
-PER = N // GROUPS
+PER = 8
+GROUPS = N // PER
 K1 = 9 * CH
 K2 = 9 * HID
 F32 = jnp.float32
@@ -64,8 +64,9 @@
 
 def kernel(
     obs, cells, counts, w1, wd, b1, w2, b2, out,
-    rows_in, meta_out, meta_in, acc, dens, edge, edge_bf, corner, corner_bf, top_in, left_in, corner_in,
-    x0, x1, xe, hid0, hid1, ext, w1v, w2v, wdf,
+    rows_in, meta_out, meta_in, acc, dens, edge, edge_bf, edge_dens, edge_fr, edge_fr_bf, corner, corner_bf,
+    top_in, left_in, corner_in, top_fr, left_fr,
+    x0, x1, xe, hid0, hid1, ext, pre_top, pre_left, w1v, w2v, wdf,
     send, recv, msend, mrecv, wsem, hsend, hrecv,
 ):
     here = position()
@@ -99,20 +100,19 @@
     w2_copy.start()
 
     lane = lax.broadcasted_iota(jnp.int32, (N, 128), 1)
-    sub = lax.broadcasted_iota(jnp.int32, (N, 128), 0)
-    column = jnp.sum(
-        jnp.where(lane == sub, jnp.broadcast_to(counts[...], (N, 128)), 0), axis=1, keepdims=True
-    )
-    cell_block = cells[...]
-    wide_cells = jnp.concatenate([cell_block] * 4, axis=1)
-    coded = jnp.where((lane & 31) < column, wide_cells, -1)
+    slot = lax.broadcasted_iota(jnp.int32, (SLOTS, N), 0)
+    coded = jnp.where(slot < counts[...], cells[...], -1)
+    coded = jnp.transpose(jnp.concatenate([coded] * 4, axis=0))
     for v in range(4):
         meta_out[v] = jnp.where((lane >> 5) == v, coded, 0).reshape(N, 1, 128)
     acc[...] = jnp.zeros_like(acc)
     dens[...] = jnp.zeros_like(dens)
     edge[...] = jnp.zeros_like(edge)
+    edge_dens[...] = jnp.zeros_like(edge_dens)
+    x1[:, pl.ds(512, 64), :] = jnp.zeros((3, 64, WIDE), BF16)
     wdf[...] = jnp.zeros_like(wdf)
-    wdf[0:9, :] = wd[...]
+    for a in range(3):
+        wdf[3 * a : 3 * a + 3, :] = wd[a]
     taps = wdf[...]
     taps_hi = taps.astype(BF16)
     taps_lo = (taps - taps_hi.astype(F32)).astype(BF16)
@@ -146,10 +146,10 @@
     def spread(v):
         return jnp.broadcast_to(v.astype(F32), (16, 128)).astype(BF16)
 
-    def codes(g):
+    def codes(start, count):
         result = []
-        for t in range(4):
-            cell = sum(meta_in[g * PER + 4 * t + u] for u in range(4))
+        for t in range(count // 4):
+            cell = sum(meta_in[start + 4 * t + u] for u in range(4))
             alive = cell >= 0
             r = cell >> 7
             c = cell & 127
@@ -172,54 +172,72 @@
             )
         return result
 
+    def across(code, which, tag, want, height):
+        return jnp.concatenate(
+            [one_hot(c[which], None if tag is None else c[tag], want, height) for c in code], axis=1
+        )
+
+    def dot_t(left, right):
+        return lax.dot_general(left, right, (((1,), (1,)), ((), ())), preferred_element_type=F32)
+
     def gather_edges(code, block):
-        wide = jnp.concatenate([block, jnp.ones((PER * SLOTS, 128), BF16)], axis=1)
+        rows = across(code, 5, None, None, 16)
+        edge_dens[0:16, :] += dot_t(rows, across(code, 4, None, None, 128))
+        last = across(code, 6, None, None, 128)
+        edge_dens[16:32, :] += dot_t(jnp.ones_like(rows), last)
         for e in range(4):
-            if e < 3:
-                hot = [one_hot(code[t][4], code[t][5], e, 128) for t in range(4)]
-            else:
-                hot = [one_hot(code[t][6], None, None, 128) for t in range(4)]
+            hot = across(code, 4, 5, e, 128) if e < 3 else last
             at = pl.ds(e * 128, 128)
-            edge[at, :] += jnp.dot(jnp.concatenate(hot, axis=1), wide, preferred_element_type=F32)
+            edge[at, :] += jnp.dot(hot, block, preferred_element_type=F32)
 
     def gather_cells(code, block):
-        lows = jnp.concatenate([one_hot(code[t][2], None, None, 128) for t in range(4)], axis=1)
-        highs = jnp.concatenate([one_hot(code[t][3], None, None, 128) for t in range(4)], axis=1)
-        dens[...] += lax.dot_general(lows, highs, (((1,), (1,)), ((), ())), preferred_element_type=F32)
+        dens[...] += dot_t(across(code, 2, None, None, 128), across(code, 3, None, None, 128))
         for b in range(16):
-            hot = jnp.concatenate([one_hot(code[t][0], code[t][1], b, 256) for t in range(4)], axis=1)
             at = pl.ds(b * 256, 256)
-            acc[at, :] += jnp.dot(hot, block, preferred_element_type=F32)
-
-    def arrived(g):
-        pltpu.make_async_copy(
-            meta_out.at[0, pl.ds(g * PER, PER)], meta_in.at[pl.ds(g * PER, PER)], mrecv.at[g]
-        ).wait()
-        pltpu.make_async_copy(
-            obs.at[pl.ds(g * PER, PER)], rows_in.at[pl.ds(g * PER, PER)], recv.at[g]
-        ).wait()
-        return codes(g), rows_in[pl.ds(g * PER, PER)].reshape(PER * SLOTS, CH)
+            acc[at, :] += jnp.dot(across(code, 0, 1, b, 256), block, preferred_element_type=F32)
+
+    def arrived(g, size):
+        start = g * PER
+        for u in range(size):
+            one = pl.ds(start + u * PER, PER)
+            pltpu.make_async_copy(meta_out.at[0, one], meta_in.at[one], mrecv.at[g + u]).wait()
+            pltpu.make_async_copy(obs.at[one], rows_in.at[one], recv.at[g + u]).wait()
+        count = size * PER
+        return codes(start, count), rows_in[pl.ds(start, count)].reshape(count * SLOTS, CH)
 
     def group(g, carry):
-        code, block = arrived(g)
+        code, block = arrived(g * 2, 2)
         gather_edges(code, block)
         gather_cells(code, block)
         return carry
 
-    lax.fori_loop(0, GROUPS - 1, group, 0)
-    code, block = arrived(GROUPS - 1)
+    lax.fori_loop(0, GROUPS // 2 - 1, group, 0)
+    code, block = arrived(GROUPS - 2, 1)
     gather_edges(code, block)
-
-    amount = edge[:, CH:]
-    scale = 1.0 / jnp.maximum(amount, 1.0)
-    edge[...] = jnp.concatenate(
-        [edge[:, 0:128] * scale, edge[:, 128:CH] * scale, amount / (1.0 + amount)], axis=1
-    )
-    edge_bf[...] = edge[...].astype(BF16)
+    gather_cells(code, block)
+    code, block = arrived(GROUPS - 1, 1)
+    gather_edges(code, block)
+
+    sub16 = lax.broadcasted_iota(jnp.int32, (16, 128), 0)
+    amount = jnp.where(sub16 == 3, edge_dens[16:32, :], edge_dens[0:16, :])
+    edge_fr_bf[...] = (amount / (1.0 + amount)).astype(BF16)
+    amount = jnp.transpose(jnp.concatenate([amount, jnp.zeros((112, 128), F32)], axis=0))
+    scales = 1.0 / jnp.maximum(amount, 1.0)
+    fractions = amount / (1.0 + amount)
+    for e in range(4):
+        scale = jnp.broadcast_to(scales[:, e : e + 1], (128, 128))
+        at = pl.ds(e * 128, 128)
+        sums = edge[at, :]
+        value = jnp.concatenate([sums[:, 0:128] * scale, sums[:, 128:CH] * scale], axis=1)
+        edge[at, :] = value
+        edge_bf[at, :] = value.astype(BF16)
+        if e < 3:
+            edge_fr[at, :] = jnp.broadcast_to(fractions[:, e : e + 1], (128, 128))
     corner[...] = jnp.zeros_like(corner)
     for a in range(3):
         for b, at in enumerate((95, 63, 127)):
-            corner[pl.ds(a * 3 + b, 1), :] = edge[pl.ds(a * 128 + at, 1), :]
+            corner[pl.ds(a * 3 + b, 1), 0:CH] = edge[pl.ds(a * 128 + at, 1), :]
+            corner[pl.ds(a * 3 + b, 1), CH:WIDE] = edge_fr[pl.ds(a * 128 + at, 1), :]
     corner_bf[...] = corner[...].astype(BF16)
     next_lat = (lat + 1) & 3
     next_lon = (lon + 1) & 31
@@ -233,6 +251,8 @@
                 (edge_bf.at[pl.ds(0, 384)], top_in, (next_lat, lon)),
                 (edge_bf.at[pl.ds(384, 96)], left_in, (lat, next_lon)),
                 (corner_bf, corner_in, (next_lat, next_lon)),
+                (edge_fr_bf, top_fr, (next_lat, lon)),
+                (edge_fr_bf, left_fr, (lat, next_lon)),
             )
         )
     ]
@@ -255,48 +275,24 @@
         if p:
             for half in range(2):
                 part = value[half * 64 : half * 64 + 64]
-                moved = jnp.concatenate([pltpu.roll(part[32:64], 1, 0), part[0:32]], axis=0)
+                moved = jnp.concatenate([down_one(part[32:64], jnp.zeros((1, WIDE), F32)), part[0:32]], axis=0)
                 x[2, pl.ds(offset(q, ip, i + half), 64), :] = moved.astype(BF16)
-
-    for halo in halos:
-        halo.wait()
-
-    inside = jnp.where(lat > 0, 1.0, 0.0).astype(F32)
-    left = left_in[...].astype(F32)
-    diag = corner_in[...].astype(F32) * inside
-    for a in range(3):
-        p0 = top_in[pl.ds(a * 128, 64), :].astype(F32) * inside
-        p1 = top_in[pl.ds(a * 128 + 64, 64), :].astype(F32) * inside
-        moved = jnp.concatenate([down_one(p1[32:64], diag[a * 3 + 2 : a * 3 + 3]), p1[0:32]], axis=0)
-        for b, top in enumerate((moved, p0, p1)):
-            side = left[b * 32 : b * 32 + 32]
-            if a == 0:
-                side = jnp.concatenate([down_one(side[24:32], diag[6 + b : 7 + b]), side[16:24]], axis=0)
-            else:
-                side = side[(a - 1) * 16 : a * 16]
-            angle = first_row(jnp.zeros((16, WIDE), F32), diag[a * 3 + b : a * 3 + b + 1])
-            top = top.astype(BF16)
-            xe[a * 3 + b, pl.ds(0, 64), :] = top
-            xe[a * 3 + b, pl.ds(64, 16), :] = side.astype(BF16)
-            xe[a * 3 + b, pl.ds(80, 16), :] = angle.astype(BF16)
-            if a == 2:
-                x1[(2, 0, 1)[b], pl.ds(512, 64), :] = top
-    for q in range(2):
-        x = x1 if q else x0
-        for ip in range(2):
-            for i in range(8):
-                at = pl.ds(offset(q, ip, i), 16)
-                t = 64 + q * 16 + ip * 8 + i
-                x[2, at, :] = first_row(x[2, at, :].astype(F32), left[t : t + 1]).astype(BF16)
 
     w1_copy.wait()
     lanes = lax.broadcasted_iota(jnp.int32, (16, 128), 1)
     tap_of_lane = jnp.where(lanes < 32, lanes & 15, 99).astype(F32).astype(BF16)
     bias1 = b1[...]
+
+    def layer_one(blocks):
+        shares = jnp.zeros((blocks[0].shape[0] // 16, 16, 128), BF16)
+        for t, data in enumerate(blocks):
+            shares = jnp.where((tap_of_lane == t)[None], data[:, CH:].reshape(-1, 16, 128), shares)
+        parts = [data[:, 0:CH] for data in blocks] + [shares.reshape(-1, 128)]
+        return jnp.dot(jnp.concatenate(parts, axis=1), w1v[...], preferred_element_type=F32)
+
     for chunk in range(4):
         ip, half = chunk >> 1, chunk & 1
-        parts = []
-        shares = None
+        blocks = []
         for a in range(3):
             for b in range(3):
                 v = (2, 0, 1)[b]
@@ -306,34 +302,92 @@
                     x, at = x1, ip * 576 + half * 256
                 else:
                     x, at = x1, (0 if ip else 512) + half * 256
-                data = x[v, pl.ds(at, 256), :]
-                if chunk == 0:
-                    data = jnp.concatenate([xe[a * 3 + b], data], axis=0)
-                parts.append(data[:, 0:CH])
-                share = data[:, CH:].reshape(-1, 16, 128)
-                if shares is None:
-                    shares = jnp.zeros_like(share)
-                shares = jnp.where((tap_of_lane == a * 3 + b)[None], share, shares)
-        parts.append(shares.reshape(-1, 128))
-        first = jnp.dot(jnp.concatenate(parts, axis=1), w1v[...], preferred_element_type=F32)
-        hidden = gelu(first + bias1)
+                blocks.append(x[v, pl.ds(at, 256), :])
+        first = layer_one(blocks) + bias1
         if chunk == 0:
-            ext[...] = hidden[0:96]
-            hidden = hidden[96:]
-            above0 = ext[pl.ds(0, 32), :] * inside
-            above1 = ext[pl.ds(32, 32), :] * inside
-            hid1[0, pl.ds(0, 32), :] = above0.astype(BF16)
-            hid1[1, pl.ds(0, 32), :] = above1.astype(BF16)
-            hid1[2, pl.ds(0, 32), :] = down_one(above1, ext[pl.ds(80, 1), :] * inside).astype(BF16)
+            pre_top[...] = first[0:64]
+        hidden = gelu(first)
         hid = hid1 if ip else hid0
         for k in range(4):
             i = half * 4 + k
+            pre_left[pl.ds(ip * 8 + i, 1), :] = first[k * 64 : k * 64 + 1]
             at = pl.ds(i * 32 + (32 if ip else 0), 32)
-            even = hidden[k * 64 : k * 64 + 32]
             odd = hidden[k * 64 + 32 : k * 64 + 64]
-            hid[0, at, :] = even.astype(BF16)
+            hid[0, at, :] = hidden[k * 64 : k * 64 + 32].astype(BF16)
             hid[1, at, :] = odd.astype(BF16)
-            hid[2, at, :] = down_one(odd, ext[pl.ds(64 + ip * 8 + i, 1), :]).astype(BF16)
+            hid[2, at, :] = pltpu.roll(odd, 1, 0).astype(BF16)
+
+    for halo in halos:
+        halo.wait()
+
+    inside = jnp.where(lat > 0, 1.0, 0.0).astype(F32)
+
+    def columns(fr):
+        return jnp.transpose(jnp.concatenate([fr[...].astype(F32), jnp.zeros((112, 128), F32)], axis=0))
+
+    top_cols = columns(top_fr)
+    left_cols = columns(left_fr)
+    left = jnp.concatenate(
+        [left_in[...].astype(F32), jnp.broadcast_to(left_cols[0:96, 3:4], (96, 128))], axis=1
+    )
+    diag = corner_in[...].astype(F32) * inside
+    for a in range(3):
+        rows = jnp.concatenate(
+            [
+                top_in[pl.ds(a * 128, 128), :].astype(F32),
+                jnp.broadcast_to(top_cols[:, a : a + 1], (128, 128)),
+            ],
+            axis=1,
+        ) * inside
+        p0, p1 = rows[0:64], rows[64:128]
+        moved = jnp.concatenate([down_one(p1[32:64], diag[a * 3 + 2 : a * 3 + 3]), p1[0:32]], axis=0)
+        for b, top in enumerate((moved, p0, p1)):
+            side = left[b * 32 : b * 32 + 32]
+            if a == 0:
+                side = jnp.concatenate([down_one(side[24:32], diag[6 + b : 7 + b]), side[16:24]], axis=0)
+            else:
+                side = side[(a - 1) * 16 : a * 16]
+            angle = first_row(jnp.zeros((16, WIDE), F32), diag[a * 3 + b : a * 3 + b + 1])
+            xe[a * 3 + b, pl.ds(0, 64), :] = top.astype(BF16)
+            xe[a * 3 + b, pl.ds(64, 16), :] = side.astype(BF16)
+            xe[a * 3 + b, pl.ds(80, 16), :] = angle.astype(BF16)
+    blocks = []
+    for a in range(3):
+        for b in range(3):
+            if a == 0:
+                over = xe[6 + b, pl.ds(0, 64), :]
+            else:
+                over = jnp.zeros((64, WIDE), BF16)
+            if b == 0:
+                side = xe[a * 3 + 2, pl.ds(64, 16), :]
+                if a == 0:
+                    side = first_row(side.astype(F32), jnp.zeros((1, WIDE), F32)).astype(BF16)
+            else:
+                side = jnp.zeros((16, WIDE), BF16)
+            blocks.append(jnp.concatenate([xe[a * 3 + b], over, side], axis=0))
+    rest = layer_one(blocks)
+    ext[...] = gelu(rest[0:96] + bias1)
+    above0 = ext[pl.ds(0, 32), :] * inside
+    above1 = ext[pl.ds(32, 32), :] * inside
+    hid1[0, pl.ds(0, 32), :] = above0.astype(BF16)
+    hid1[1, pl.ds(0, 32), :] = above1.astype(BF16)
+    hid1[2, pl.ds(0, 32), :] = down_one(above1, ext[pl.ds(80, 1), :] * inside).astype(BF16)
+    side = rest[160:176]
+    over = rest[96:160] + first_row(jnp.zeros((64, HID), F32), side[0:1])
+    over = gelu(pre_top[...] + over)
+    side = gelu(pre_left[...] + side)
+    hid0[0, pl.ds(0, 32), :] = over[0:32].astype(BF16)
+    hid0[1, pl.ds(0, 32), :] = over[32:64].astype(BF16)
+    hid0[2, pl.ds(0, 32), :] = down_one(over[32:64], ext[pl.ds(64, 1), :]).astype(BF16)
+    for ip in range(2):
+        hid = hid1 if ip else hid0
+        for i in range(8):
+            n = ip * 8 + i
+            if n == 0:
+                continue
+            at = pl.ds(i * 32 + (32 if ip else 0), 16)
+            hid[0, at, :] = first_row(hid[0, at, :].astype(F32), side[n : n + 1]).astype(BF16)
+            hid[2, at, :] = first_row(hid[2, at, :].astype(F32), ext[pl.ds(64 + n, 1), :]).astype(BF16)
 
     w2_copy.wait()
     parts = []
@@ -368,19 +422,26 @@
             pltpu.VMEM((N, 1, 128), jnp.int32),
             pltpu.VMEM((4096, CH), F32),
             pltpu.VMEM((128, 128), F32),
-            pltpu.VMEM((512, WIDE), F32),
-            pltpu.VMEM((512, WIDE), BF16),
+            pltpu.VMEM((512, CH), F32),
+            pltpu.VMEM((512, CH), BF16),
+            pltpu.VMEM((32, 128), F32),
+            pltpu.VMEM((384, 128), F32),
+            pltpu.VMEM((16, 128), BF16),
             pltpu.VMEM((16, WIDE), F32),
             pltpu.VMEM((16, WIDE), BF16),
-            pltpu.VMEM((384, WIDE), BF16),
-            pltpu.VMEM((96, WIDE), BF16),
+            pltpu.VMEM((384, CH), BF16),
+            pltpu.VMEM((96, CH), BF16),
             pltpu.VMEM((16, WIDE), BF16),
+            pltpu.VMEM((16, 128), BF16),
+            pltpu.VMEM((16, 128), BF16),
             pltpu.VMEM((3, 1024, WIDE), BF16),
             pltpu.VMEM((3, 1088, WIDE), BF16),
             pltpu.VMEM((9, 96, WIDE), BF16),
             pltpu.VMEM((3, 256, HID), BF16),
             pltpu.VMEM((3, 288, HID), BF16),
             pltpu.VMEM((96, HID), F32),
+            pltpu.VMEM((64, HID), F32),
+            pltpu.VMEM((16, HID), F32),
             pltpu.VMEM((K1 + 128, HID), BF16),
             pltpu.VMEM((K2, HID), BF16),
             pltpu.VMEM((16, HID), F32),
@@ -389,18 +450,18 @@
             dma,
             dma((GROUPS,)),
             dma((2,)),
-            dma((3,)),
-            dma((3,)),
+            dma((5,)),
+            dma((5,)),
         ],
         compiler_params=pltpu.CompilerParams(
             collective_id=0, has_side_effects=True, vmem_limit_bytes=56 * 2**20
         ),
     )(
         obs,
-        cells,
+        cells.T,
         counts.reshape(1, N),
         conv_in.reshape(K1, HID),
-        conv_density.reshape(9, HID),
+        conv_density,
         bias_in.reshape(1, HID),
         conv_mid.reshape(K2, HID),
         bias_mid.reshape(1, HID),

time: 58 us -> 51.4 us (0.89); the launches traced: 56.8 us -> 51.2 us
  local copies, waits for them, and re-layouts: 4.46 us -> 1.67 us
  Pallas kernels: 52.3 us -> 49.6 us
    pallas_call x1, Pallas kernels: 52.3 us -> 49.6 us  [on_device(): pl.pallas_call(kernel, out_shape=jax.ShapeDtypeStruct((8, 32, HID), BF16)...]
    unnamed x2 -> x1, local copies, waits for them, and re-layouts: 3.12 us -> 1.67 us
    reshape x1 -> x0, local copies, waits for them, and re-layouts: 1.35 us -> none  [on_device(): conv_density.reshape(9, HID)]
where the time goes in v2:
time: 51.4 us; the launch traced here: 51.2 us
  Pallas kernels  49.6 us (96%)
  local copies, waits for them, and re-layouts  1.67 us (3%)
    pallas_call x1, Pallas kernels, on_device(): pl.pallas_call(kernel, out_shape=jax.ShapeDtypeStruct((8, 32, HID), BF16)...  49.6 us
    unnamed x1, local copies, waits for them, and re-layouts  1.67 us

profile of v2, /device:TPU:1, one launch (start us, length us, event | category | flops | bytes accessed | tf_op | source)
XLA Modules:
  0.0 51.2 jit_solution(18345088041778446807)
XLA Ops:
  0.0 49.6 %shard_map.82 = bf16[8,32,512]{2,1,0:T(8,128)(2,1)} custom-call(bf16[128,32,256]{2,1,0:T(8,128)(2,1)} %obs.1, s32[32,128]{1,0:T(8,128)} %bitcast.8, s32[1,128]{1,0:T(1,128)} %bitcast.11, bf16[2304,512]{1,0:T(8,128)(2,1)} %bitcast.7, f32[3,3,512]{2,1,0:T(4,128)} %wd.1, f32[1,512]{1,0:T(1,128)} %bitcast.9, bf16[4608,512]{1,0:T(8,128)(2,1)} %bitcast.6, ...), custom_call_target="tpu_custom_call" | custom-call | tf_op jit(solution)/shard_map/pallas_call | solution.py:414
  49.6 1.7 %copy.10 = bf16[8,32,512]{2,1,0:T(8,128)(2,1)} copy(bf16[8,32,512]{2,1,0:T(8,128)(2,1)} %shard_map.82) | data formatting | bytes 524288

commit v3 on v2

--- a/solution.py
+++ b/solution.py
@@ -27,13 +27,12 @@
     return lon & 3, ((lat >> 1) << 1) + (lon >> 4), (lon >> 2) & 3, lat & 1
 
 
-def partner(here, bb, cc, aa, dc, sign):
-    x, y, z, core = here
-    x = (x + sign * aa) & 3
-    y = (y + sign * (aa + bb)) & 3
-    z = (z + sign * (aa + cc)) & 3
-    core = core ^ dc
-    return (y & 2) + core, ((y & 1) << 4) + (z << 2) + x
+def around(v, d):
+    return (v + d) & 3
+
+
+def wrapped(v):
+    return jnp.where(v > 2, v - 2, v + 1) if not isinstance(v, int) else v % 3 + 1
 
 
 def gelu(x):
@@ -67,33 +66,28 @@
     rows_in, meta_out, meta_in, acc, dens, edge, edge_bf, edge_dens, edge_fr, edge_fr_bf, corner, corner_bf,
     top_in, left_in, corner_in, top_fr, left_fr,
     x0, x1, xe, hid0, hid1, ext, pre_top, pre_left, w1v, w2v, wdf,
-    send, recv, msend, mrecv, wsem, hsend, hrecv,
+    entered, send, recv, msend, mrecv, wsem, hsend, hrecv,
 ):
-    here = position()
+    x_me, y_me, z_me, core_me = position()
     lat = lax.axis_index("lat")
     lon = lax.axis_index("lon")
 
-    def each(fn):
-        for i in range(8):
-            fn(i, 0, 0, i >> 1, i & 1)
-
-        def body(o, carry):
-            for i in range(8):
-                fn(o * 8 + i, o >> 2, o & 3, i >> 1, i & 1)
-            return carry
-
-        lax.fori_loop(1, 16, body, 0)
+    def device(dx, dy, dz, dc):
+        y = around(y_me, dy)
+        core = core_me ^ dc
+        return (y & 2) + core, ((y & 1) << 4) + (around(z_me, dz) << 2) + around(x_me, dx)
+
+    def signal(sem, offsets):
+        for to in offsets:
+            pl.semaphore_signal(sem, inc=1, device_id=device(*to), device_id_type=MESH)
 
     barrier = pltpu.get_barrier_semaphore()
-
-    def greet(k, bb, cc, aa, dc):
-        if isinstance(k, int) and k == 0:
-            return
-        pl.semaphore_signal(
-            barrier, inc=1, device_id=partner(here, bb, cc, aa, dc, -1), device_id_type=MESH
-        )
-
-    each(greet)
+    steps = (1, 2, 3)
+    x_line = [(d, 0, 0, 0) for d in steps]
+    y_line = [(0, d, 0, 0) for d in steps]
+    z_line = [(0, 0, d, 0) for d in steps]
+    lines = [(0, 0, 0, 1)] + [o[:3] + (c,) for o in x_line + y_line + z_line for c in (0, 1)]
+    signal(barrier, lines)
     w1_copy = pltpu.make_async_copy(w1, w1v.at[pl.ds(0, K1)], wsem.at[0])
     w2_copy = pltpu.make_async_copy(w2, w2v, wsem.at[1])
     w1_copy.start()
@@ -120,28 +114,66 @@
         [taps_hi, taps_lo, jnp.zeros((96, HID), BF16)], axis=0
     )
 
-    pl.semaphore_wait(barrier, N - 1)
-
-    def dispatch(k, bb, cc, aa, dc):
-        to_lat, to_lon = partner(here, bb, cc, aa, dc, 1)
+    def dispatch(k, dx, dy, dz, dc):
+        to_lat, to_lon = device(dx, dy, dz, dc)
         to = to_lat * 32 + to_lon
-        v = (aa * 2 + dc) & 3
+        src_meta, src = meta_out.at[k & 3, pl.ds(to, 1)], obs.at[pl.ds(to, 1)]
+        dst_meta, dst = meta_in.at[pl.ds(k, 1)], rows_in.at[pl.ds(k, 1)]
         if isinstance(k, int) and k == 0:
-            pltpu.make_async_copy(meta_out.at[v, pl.ds(to, 1)], meta_in.at[pl.ds(0, 1)], mrecv.at[0]).start()
-            pltpu.make_async_copy(obs.at[pl.ds(to, 1)], rows_in.at[pl.ds(0, 1)], recv.at[0]).start()
+            pltpu.make_async_copy(src_meta, dst_meta, mrecv.at[0]).start()
+            pltpu.make_async_copy(src, dst, recv.at[0]).start()
             return
+        to = (to_lat, to_lon)
         pltpu.make_async_remote_copy(
-            src_ref=meta_out.at[v, pl.ds(to, 1)], dst_ref=meta_in.at[pl.ds(k, 1)],
-            send_sem=msend, recv_sem=mrecv.at[k // PER],
-            device_id=(to_lat, to_lon), device_id_type=MESH,
+            src_ref=src_meta, dst_ref=dst_meta, send_sem=msend, recv_sem=mrecv.at[k >> 3],
+            device_id=to, device_id_type=MESH,
         ).start()
         pltpu.make_async_remote_copy(
-            src_ref=obs.at[pl.ds(to, 1)], dst_ref=rows_in.at[pl.ds(k, 1)],
-            send_sem=send, recv_sem=recv.at[k // PER],
-            device_id=(to_lat, to_lon), device_id_type=MESH,
+            src_ref=src, dst_ref=dst, send_sem=send, recv_sem=recv.at[k >> 3],
+            device_id=to, device_id_type=MESH,
         ).start()
 
-    each(dispatch)
+    pl.semaphore_wait(barrier, len(lines))
+    signal(entered.at[0], y_line)
+    signal(entered.at[1], z_line)
+    signal(entered.at[2], z_line)
+    dispatch(0, 0, 0, 0, 0)
+    dispatch(1, 0, 0, 0, 1)
+
+    def along_lines(b, carry):
+        for axis in range(3):
+            for dc in range(2):
+                d = [0, 0, 0]
+                d[axis] = b + 1
+                dispatch(2 + b * 6 + axis * 2 + dc, *d, dc)
+        return carry
+
+    def along_planes(b, carry):
+        for a in range(3):
+            for plane in range(3):
+                for dc in range(2):
+                    d = [a + 1, wrapped(a + b)]
+                    d.insert(2 - plane, 0)
+                    dispatch(20 + b * 18 + a * 6 + plane * 2 + dc, *d, dc)
+        return carry
+
+    def elsewhere(b, carry):
+        for c in range(3):
+            for a in range(3):
+                for dc in range(2):
+                    dispatch(
+                        74 + b * 18 + c * 6 + a * 2 + dc, a + 1, wrapped(a + b), wrapped(a + c), dc
+                    )
+        return carry
+
+    lax.fori_loop(0, 3, along_lines, 0)
+    pl.semaphore_wait(entered.at[0], 3)
+    signal(entered.at[3], z_line)
+    pl.semaphore_wait(entered.at[1], 3)
+    pl.semaphore_wait(entered.at[2], 3)
+    lax.fori_loop(0, 3, along_planes, 0)
+    pl.semaphore_wait(entered.at[3], 3)
+    lax.fori_loop(0, 3, elsewhere, 0)
 
     def spread(v):
         return jnp.broadcast_to(v.astype(F32), (16, 128)).astype(BF16)
@@ -445,6 +477,7 @@
             pltpu.VMEM((K1 + 128, HID), BF16),
             pltpu.VMEM((K2, HID), BF16),
             pltpu.VMEM((16, HID), F32),
+            pltpu.SemaphoreType.REGULAR((4,)),
             dma,
             dma((GROUPS,)),
             dma,

time: 51.4 us -> 48.1 us (0.936)
  Pallas kernels: 49.6 us -> 46.2 us
    pallas_call x1, Pallas kernels: 49.6 us -> 46.2 us  [on_device(): pl.pallas_call(kernel, out_shape=jax.ShapeDtypeStruct((8, 32, HID), BF16)...]
where the time goes in v3:
time: 48.1 us; the launch traced here: 47.9 us
  Pallas kernels  46.2 us (96%)
  local copies, waits for them, and re-layouts  1.67 us (3%)
    pallas_call x1, Pallas kernels, on_device(): pl.pallas_call(kernel, out_shape=jax.ShapeDtypeStruct((8, 32, HID), BF16)...  46.2 us
    unnamed x1, local copies, waits for them, and re-layouts  1.67 us

profile of v3, /device:TPU:1, one launch (start us, length us, event | category | flops | bytes accessed | tf_op | source)
XLA Modules:
  0.0 47.9 jit_solution(8894221623510600585)
XLA Ops:
  0.0 46.2 %shard_map.82 = bf16[8,32,512]{2,1,0:T(8,128)(2,1)} custom-call(bf16[128,32,256]{2,1,0:T(8,128)(2,1)} %obs.1, s32[32,128]{1,0:T(8,128)} %bitcast.8, s32[1,128]{1,0:T(1,128)} %bitcast.11, bf16[2304,512]{1,0:T(8,128)(2,1)} %bitcast.7, f32[3,3,512]{2,1,0:T(4,128)} %wd.1, f32[1,512]{1,0:T(1,128)} %bitcast.9, bf16[4608,512]{1,0:T(8,128)(2,1)} %bitcast.6, ...), custom_call_target="tpu_custom_call" | custom-call | tf_op jit(solution)/shard_map/pallas_call | solution.py:446
  46.2 1.7 %copy.10 = bf16[8,32,512]{2,1,0:T(8,128)(2,1)} copy(bf16[8,32,512]{2,1,0:T(8,128)(2,1)} %shard_map.82) | data formatting | bytes 524288

commit v4 on v3

--- a/solution.py
+++ b/solution.py
@@ -62,12 +62,19 @@
 
 
 def kernel(
-    obs, cells, counts, w1, wd, b1, w2, b2, out,
+    obs, cells_in, counts_in, w1, wd_in, b1_in, w2, hid0, hid1, w2v,
+    cells, counts, wd, b1,
     rows_in, meta_out, meta_in, acc, dens, edge, edge_bf, edge_dens, edge_fr, edge_fr_bf, corner, corner_bf,
     top_in, left_in, corner_in, top_fr, left_fr,
-    x0, x1, xe, hid0, hid1, ext, pre_top, pre_left, w1v, w2v, wdf,
-    entered, send, recv, msend, mrecv, wsem, hsend, hrecv,
+    x0, x1, xe, ext, pre_top, pre_left, w1v, wdf,
+    entered, send, recv, msend, mrecv, wsem, ssem, hsend, hrecv,
 ):
+    small = [
+        pltpu.make_async_copy(src, dst, ssem.at[i])
+        for i, (src, dst) in enumerate(((cells_in, cells), (counts_in, counts), (wd_in, wd), (b1_in, b1)))
+    ]
+    for copy in small:
+        copy.start()
     x_me, y_me, z_me, core_me = position()
     lat = lax.axis_index("lat")
     lon = lax.axis_index("lon")
@@ -90,9 +97,11 @@
     signal(barrier, lines)
     w1_copy = pltpu.make_async_copy(w1, w1v.at[pl.ds(0, K1)], wsem.at[0])
     w2_copy = pltpu.make_async_copy(w2, w2v, wsem.at[1])
+    w2_copy.start()
     w1_copy.start()
-    w2_copy.start()
-
+
+    for copy in small:
+        copy.wait()
     lane = lax.broadcasted_iota(jnp.int32, (N, 128), 1)
     slot = lax.broadcasted_iota(jnp.int32, (SLOTS, N), 0)
     coded = jnp.where(slot < counts[...], cells[...], -1)
@@ -149,18 +158,18 @@
         return carry
 
     def along_planes(b, carry):
-        for a in range(3):
-            for plane in range(3):
-                for dc in range(2):
+        for dc in range(2):
+            for a in range(3):
+                for plane in range(3):
                     d = [a + 1, wrapped(a + b)]
                     d.insert(2 - plane, 0)
                     dispatch(20 + b * 18 + a * 6 + plane * 2 + dc, *d, dc)
         return carry
 
     def elsewhere(b, carry):
-        for c in range(3):
-            for a in range(3):
-                for dc in range(2):
+        for dc in range(2):
+            for c in range(3):
+                for a in range(3):
                     dispatch(
                         74 + b * 18 + c * 6 + a * 2 + dc, a + 1, wrapped(a + b), wrapped(a + c), dc
                     )
@@ -422,6 +431,13 @@
             hid[2, at, :] = first_row(hid[2, at, :].astype(F32), ext[pl.ds(64 + n, 1), :]).astype(BF16)
 
     w2_copy.wait()
+    pltpu.make_async_copy(obs.at[pl.ds(1, N - 1)], rows_in.at[pl.ds(1, N - 1)], send).wait()
+    pltpu.make_async_copy(
+        meta_out.at[0, pl.ds(1, N - 1)], meta_in.at[pl.ds(1, N - 1)], msend
+    ).wait()
+
+
+def layer_two(hid0, hid1, w2, b2, out):
     parts = []
     for a in range(3):
         for b in range(3):
@@ -430,25 +446,28 @@
                 parts.append(hid0[v])
             else:
                 parts.append(hid1[v, pl.ds(32 if a == 2 else 0, 256), :])
-    second = jnp.dot(jnp.concatenate(parts, axis=1), w2v[...], preferred_element_type=F32)
+    second = jnp.dot(jnp.concatenate(parts, axis=1), w2[...], preferred_element_type=F32)
     out[...] = gelu(second + b2[...]).astype(BF16).reshape(8, 32, HID)
-
-    pltpu.make_async_copy(obs.at[pl.ds(1, N - 1)], rows_in.at[pl.ds(1, N - 1)], send).wait()
-    pltpu.make_async_copy(
-        meta_out.at[0, pl.ds(1, N - 1)], meta_in.at[pl.ds(1, N - 1)], msend
-    ).wait()
 
 
 def on_device(obs, cells, counts, conv_in, conv_density, bias_in, conv_mid, bias_mid):
     vmem = pl.BlockSpec(memory_space=pltpu.VMEM)
-    hbm = pl.BlockSpec(memory_space=pl.ANY)
+    hbm = pl.BlockSpec(memory_space=pltpu.HBM)
     dma = pltpu.SemaphoreType.DMA
-    return pl.pallas_call(
+    hid0, hid1, w2 = pl.pallas_call(
         kernel,
-        out_shape=jax.ShapeDtypeStruct((8, 32, HID), BF16),
-        in_specs=[hbm, vmem, vmem, hbm, vmem, vmem, hbm, vmem],
-        out_specs=vmem,
+        out_shape=[
+            pltpu.VMEM((3, 256, HID), BF16),
+            pltpu.VMEM((3, 288, HID), BF16),
+            pltpu.VMEM((K2, HID), BF16),
+        ],
+        in_specs=[hbm] * 7,
+        out_specs=[vmem, vmem, vmem],
         scratch_shapes=[
+            pltpu.VMEM((SLOTS, N), jnp.int32),
+            pltpu.VMEM((1, N), jnp.int32),
+            pltpu.VMEM((3, 3, HID), F32),
+            pltpu.VMEM((1, HID), F32),
             pltpu.VMEM((N, SLOTS, CH), BF16),
             pltpu.VMEM((4, N, 1, 128), jnp.int32),
             pltpu.VMEM((N, 1, 128), jnp.int32),
@@ -469,13 +488,10 @@
             pltpu.VMEM((3, 1024, WIDE), BF16),
             pltpu.VMEM((3, 1088, WIDE), BF16),
             pltpu.VMEM((9, 96, WIDE), BF16),
-            pltpu.VMEM((3, 256, HID), BF16),
-            pltpu.VMEM((3, 288, HID), BF16),
             pltpu.VMEM((96, HID), F32),
             pltpu.VMEM((64, HID), F32),
             pltpu.VMEM((16, HID), F32),
             pltpu.VMEM((K1 + 128, HID), BF16),
-            pltpu.VMEM((K2, HID), BF16),
             pltpu.VMEM((16, HID), F32),
             pltpu.SemaphoreType.REGULAR((4,)),
             dma,
@@ -483,11 +499,12 @@
             dma,
             dma((GROUPS,)),
             dma((2,)),
+            dma((4,)),
             dma((5,)),
             dma((5,)),
         ],
         compiler_params=pltpu.CompilerParams(
-            collective_id=0, has_side_effects=True, vmem_limit_bytes=56 * 2**20
+            collective_id=0, has_side_effects=True, vmem_limit_bytes=54 * 2**20
         ),
     )(
         obs,
@@ -497,8 +514,14 @@
         conv_density,
         bias_in.reshape(1, HID),
         conv_mid.reshape(K2, HID),
-        bias_mid.reshape(1, HID),
     )
+    return pl.pallas_call(
+        layer_two,
+        out_shape=jax.ShapeDtypeStruct((8, 32, HID), BF16),
+        in_specs=[vmem, vmem, vmem, vmem],
+        out_specs=vmem,
+        compiler_params=pltpu.CompilerParams(vmem_limit_bytes=20 * 2**20),
+    )(hid0, hid1, w2, bias_mid.reshape(1, HID))
 
 
 def solution(mesh):

time: 48.1 us -> 45.7 us (0.950)
  local copies, waits for them, and re-layouts: 1.67 us -> 0.01 us
  Pallas kernels: 46.2 us -> 45.6 us
    unnamed x1 -> x2, local copies, waits for them, and re-layouts: 1.67 us -> 0.01 us
    pallas_call x1 -> x2, Pallas kernels: 46.2 us -> 45.6 us  [the longest x1 43.4 us: on_device(): pl.pallas_call(kernel, out_shape=[pltpu.VMEM((3, 256, HID), BF16), pltpu....]
where the time goes in v4:
time: 45.7 us; the launch traced here: 45.6 us
  Pallas kernels  45.6 us (100%)
    pallas_call x1, Pallas kernels, on_device(): pl.pallas_call(kernel, out_shape=[pltpu.VMEM((3, 256, HID), BF16), pltpu....  43.4 us
    pallas_call x1, Pallas kernels, on_device(): pl.pallas_call(layer_two, out_shape=jax.ShapeDtypeStruct((8, 32, HID), BF...  2.2 us

profile of v4, /device:TPU:1, one launch (start us, length us, event | category | flops | bytes accessed | tf_op | source)
XLA Modules:
  0.0 45.6 jit_solution(6274777614192758358)
XLA Ops:
  0.0 0.0 copy-start
  0.0 43.4 %shard_map.82 = (bf16[3,256,512]{2,1,0:T(8,128)(2,1)S(1)}, bf16[3,288,512]{2,1,0:T(8,128)(2,1)S(1)}, bf16[4608,512]{1,0:T(8,128)(2,1)S(1)}) custom-call(bf16[128,32,256]{2,1,0:T(8,128)(2,1)} %obs.1, s32[32,128]{1,0:T(8,128)} %bitcast.9, s32[1,128]{1,0:T(1,128)} %bitcast.11, bf16[2304,512]{1,0:T(8,128)(2,1)} %bitcast.8, f32[3,3,512]{2,1,0:T(4,128)} %wd_in.1, ...), custom_call_target="tpu_custom_call" | custom-call | tf_op jit(solution)/shard_map/pallas_call | solution.py:457
  43.4 0.0 copy-done
  43.4 2.2 %shard_map.83 = bf16[8,32,512]{2,1,0:T(8,128)(2,1)} custom-call(bf16[3,256,512]{2,1,0:T(8,128)(2,1)S(1)} %get-tuple-element.8.hid0, bf16[3,288,512]{2,1,0:T(8,128)(2,1)S(1)} %get-tuple-element.9.hid1, bf16[4608,512]{1,0:T(8,128)(2,1)S(1)} %get-tuple-element.10.w2, f32[1,512]{1,0:T(1,128)S(1)} %bitcast.6), custom_call_target="tpu_custom_call" | custom-call | tf_op jit(solution)/shard_map/pallas_call | solution.py:518
Async XLA Ops:
  0.0 43.4 %copy-start = (f32[512]{0:T(512)S(1)}, f32[512]{0:T(512)}, u32[]{:S(2)}) copy-start(f32[512]{0:T(512)} %param.15) | copy-start | bytes 6148

commit v5 on v4

--- a/solution.py
+++ b/solution.py
@@ -108,6 +108,12 @@
     coded = jnp.transpose(jnp.concatenate([coded] * 4, axis=0))
     for v in range(4):
         meta_out[v] = jnp.where((lane >> 5) == v, coded, 0).reshape(N, 1, 128)
+
+    @pl.when(lat == 0)
+    def _():
+        for ref in (top_in, corner_in, top_fr):
+            ref[...] = jnp.zeros_like(ref)
+
     acc[...] = jnp.zeros_like(acc)
     dens[...] = jnp.zeros_like(dens)
     edge[...] = jnp.zeros_like(edge)
@@ -297,8 +303,14 @@
             )
         )
     ]
-    for halo in halos:
+    tops, lefts = (halos[0], halos[2], halos[3]), (halos[1], halos[4])
+    for halo in lefts:
         halo.start()
+
+    @pl.when(lat < 3)
+    def _():
+        for halo in tops:
+            halo.start()
 
     gather_cells(code, block)
 
@@ -358,8 +370,18 @@
             hid[1, at, :] = odd.astype(BF16)
             hid[2, at, :] = pltpu.roll(odd, 1, 0).astype(BF16)
 
-    for halo in halos:
+    for halo in lefts:
         halo.wait()
+
+    @pl.when(lat < 3)
+    def _():
+        for halo in tops:
+            halo.wait_send()
+
+    @pl.when(lat > 0)
+    def _():
+        for halo in tops:
+            halo.wait_recv()
 
     inside = jnp.where(lat > 0, 1.0, 0.0).astype(F32)
 

time: 45.7 us -> 45.6 us (level)
  no operation moved by 1% of the time
where the time goes in v5:
time: 45.6 us; the launch traced here: 45.5 us
  Pallas kernels  45.5 us (100%)
    pallas_call x1, Pallas kernels, on_device(): pl.pallas_call(kernel, out_shape=[pltpu.VMEM((3, 256, HID), BF16), pltpu....  43.3 us
    pallas_call x1, Pallas kernels, on_device(): pl.pallas_call(layer_two, out_shape=jax.ShapeDtypeStruct((8, 32, HID), BF...  2.2 us

profile of v5, /device:TPU:1, one launch (start us, length us, event | category | flops | bytes accessed | tf_op | source)
XLA Modules:
  0.0 45.5 jit_solution(17283628445579929996)
XLA Ops:
  0.0 0.0 copy-start
  0.0 43.3 %shard_map.82 = (bf16[3,256,512]{2,1,0:T(8,128)(2,1)S(1)}, bf16[3,288,512]{2,1,0:T(8,128)(2,1)S(1)}, bf16[4608,512]{1,0:T(8,128)(2,1)S(1)}) custom-call(bf16[128,32,256]{2,1,0:T(8,128)(2,1)} %obs.1, s32[32,128]{1,0:T(8,128)} %bitcast.9, s32[1,128]{1,0:T(1,128)} %bitcast.11, bf16[2304,512]{1,0:T(8,128)(2,1)} %bitcast.8, f32[3,3,512]{2,1,0:T(4,128)} %wd_in.1, ...), custom_call_target="tpu_custom_call" | custom-call | tf_op jit(solution)/shard_map/pallas_call | solution.py:479
  43.3 0.0 copy-done
  43.3 2.2 %shard_map.83 = bf16[8,32,512]{2,1,0:T(8,128)(2,1)} custom-call(bf16[3,256,512]{2,1,0:T(8,128)(2,1)S(1)} %get-tuple-element.8.hid0, bf16[3,288,512]{2,1,0:T(8,128)(2,1)S(1)} %get-tuple-element.9.hid1, bf16[4608,512]{1,0:T(8,128)(2,1)S(1)} %get-tuple-element.10.w2, f32[1,512]{1,0:T(1,128)S(1)} %bitcast.6), custom_call_target="tpu_custom_call" | custom-call | tf_op jit(solution)/shard_map/pallas_call | solution.py:540
Async XLA Ops:
  0.0 43.3 %copy-start = (f32[512]{0:T(512)S(1)}, f32[512]{0:T(512)}, u32[]{:S(2)}) copy-start(f32[512]{0:T(512)} %param.15) | copy-start | bytes 6148

commit v6 on v5

--- a/solution.py
+++ b/solution.py
@@ -468,8 +468,11 @@
                 parts.append(hid0[v])
             else:
                 parts.append(hid1[v, pl.ds(32 if a == 2 else 0, 256), :])
-    second = jnp.dot(jnp.concatenate(parts, axis=1), w2[...], preferred_element_type=F32)
-    out[...] = gelu(second + b2[...]).astype(BF16).reshape(8, 32, HID)
+    taps = jnp.concatenate(parts, axis=1)
+    for n in range(2):
+        at = pl.ds(n * 256, 256)
+        second = jnp.dot(taps, w2[:, at], preferred_element_type=F32)
+        out[:, :, at] = gelu(second + b2[:, at]).astype(BF16).reshape(8, 32, 256)
 
 
 def on_device(obs, cells, counts, conv_in, conv_density, bias_in, conv_mid, bias_mid):

time: 45.6 us -> 45.6 us (level)
  no operation moved by 1% of the time
where the time goes in v6:
time: 45.6 us; the launch traced here: 45.5 us
  Pallas kernels  45.5 us (100%)
    pallas_call x1, Pallas kernels, on_device(): pl.pallas_call(kernel, out_shape=[pltpu.VMEM((3, 256, HID), BF16), pltpu....  43.3 us
    pallas_call x1, Pallas kernels, on_device(): pl.pallas_call(layer_two, out_shape=jax.ShapeDtypeStruct((8, 32, HID), BF...  2.2 us

profile of v6, /device:TPU:1, one launch (start us, length us, event | category | flops | bytes accessed | tf_op | source)
XLA Modules:
  0.0 45.5 jit_solution(17283628445579929996)
XLA Ops:
  0.0 0.0 copy-start
  0.0 43.3 %shard_map.82 = (bf16[3,256,512]{2,1,0:T(8,128)(2,1)S(1)}, bf16[3,288,512]{2,1,0:T(8,128)(2,1)S(1)}, bf16[4608,512]{1,0:T(8,128)(2,1)S(1)}) custom-call(bf16[128,32,256]{2,1,0:T(8,128)(2,1)} %obs.1, s32[32,128]{1,0:T(8,128)} %bitcast.9, s32[1,128]{1,0:T(1,128)} %bitcast.11, bf16[2304,512]{1,0:T(8,128)(2,1)} %bitcast.8, f32[3,3,512]{2,1,0:T(4,128)} %wd_in.1, ...), custom_call_target="tpu_custom_call" | custom-call | tf_op jit(solution)/shard_map/pallas_call | solution.py:482
  43.3 0.0 copy-done
  43.3 2.2 %shard_map.83 = bf16[8,32,512]{2,1,0:T(8,128)(2,1)} custom-call(bf16[3,256,512]{2,1,0:T(8,128)(2,1)S(1)} %get-tuple-element.8.hid0, bf16[3,288,512]{2,1,0:T(8,128)(2,1)S(1)} %get-tuple-element.9.hid1, bf16[4608,512]{1,0:T(8,128)(2,1)S(1)} %get-tuple-element.10.w2, f32[1,512]{1,0:T(1,128)S(1)} %bitcast.6), custom_call_target="tpu_custom_call" | custom-call | tf_op jit(solution)/shard_map/pallas_call | solution.py:543
Async XLA Ops:
  0.0 43.3 %copy-start = (f32[512]{0:T(512)S(1)}, f32[512]{0:T(512)}, u32[]{:S(2)}) copy-start(f32[512]{0:T(512)} %param.15) | copy-start | bytes 6148

commit v7 on v5

--- a/solution.py
+++ b/solution.py
@@ -108,26 +108,6 @@
     coded = jnp.transpose(jnp.concatenate([coded] * 4, axis=0))
     for v in range(4):
         meta_out[v] = jnp.where((lane >> 5) == v, coded, 0).reshape(N, 1, 128)
-
-    @pl.when(lat == 0)
-    def _():
-        for ref in (top_in, corner_in, top_fr):
-            ref[...] = jnp.zeros_like(ref)
-
-    acc[...] = jnp.zeros_like(acc)
-    dens[...] = jnp.zeros_like(dens)
-    edge[...] = jnp.zeros_like(edge)
-    edge_dens[...] = jnp.zeros_like(edge_dens)
-    x1[:, pl.ds(512, 64), :] = jnp.zeros((3, 64, WIDE), BF16)
-    wdf[...] = jnp.zeros_like(wdf)
-    for a in range(3):
-        wdf[3 * a : 3 * a + 3, :] = wd[a]
-    taps = wdf[...]
-    taps_hi = taps.astype(BF16)
-    taps_lo = (taps - taps_hi.astype(F32)).astype(BF16)
-    w1v[pl.ds(K1, 128), :] = jnp.concatenate(
-        [taps_hi, taps_lo, jnp.zeros((96, HID), BF16)], axis=0
-    )
 
     def dispatch(k, dx, dy, dz, dc):
         to_lat, to_lon = device(dx, dy, dz, dc)
@@ -189,6 +169,26 @@
     lax.fori_loop(0, 3, along_planes, 0)
     pl.semaphore_wait(entered.at[3], 3)
     lax.fori_loop(0, 3, elsewhere, 0)
+
+    @pl.when(lat == 0)
+    def _():
+        for ref in (top_in, corner_in, top_fr):
+            ref[...] = jnp.zeros_like(ref)
+
+    acc[...] = jnp.zeros_like(acc)
+    dens[...] = jnp.zeros_like(dens)
+    edge[...] = jnp.zeros_like(edge)
+    edge_dens[...] = jnp.zeros_like(edge_dens)
+    x1[:, pl.ds(512, 64), :] = jnp.zeros((3, 64, WIDE), BF16)
+    wdf[...] = jnp.zeros_like(wdf)
+    for a in range(3):
+        wdf[3 * a : 3 * a + 3, :] = wd[a]
+    taps = wdf[...]
+    taps_hi = taps.astype(BF16)
+    taps_lo = (taps - taps_hi.astype(F32)).astype(BF16)
+    w1v[pl.ds(K1, 128), :] = jnp.concatenate(
+        [taps_hi, taps_lo, jnp.zeros((96, HID), BF16)], axis=0
+    )
 
     def spread(v):
         return jnp.broadcast_to(v.astype(F32), (16, 128)).astype(BF16)

time: 45.6 us -> 45.6 us (level)
  no operation moved by 1% of the time
where the time goes in v7:
time: 45.6 us; the launch traced here: 45.5 us
  Pallas kernels  45.5 us (100%)
    pallas_call x1, Pallas kernels, on_device(): pl.pallas_call(kernel, out_shape=[pltpu.VMEM((3, 256, HID), BF16), pltpu....  43.3 us
    pallas_call x1, Pallas kernels, on_device(): pl.pallas_call(layer_two, out_shape=jax.ShapeDtypeStruct((8, 32, HID), BF...  2.2 us

profile of v7, /device:TPU:1, one launch (start us, length us, event | category | flops | bytes accessed | tf_op | source)
XLA Modules:
  0.0 45.5 jit_solution(16776475591671138748)
XLA Ops:
  0.0 0.0 copy-start
  0.0 43.3 %shard_map.82 = (bf16[3,256,512]{2,1,0:T(8,128)(2,1)S(1)}, bf16[3,288,512]{2,1,0:T(8,128)(2,1)S(1)}, bf16[4608,512]{1,0:T(8,128)(2,1)S(1)}) custom-call(bf16[128,32,256]{2,1,0:T(8,128)(2,1)} %obs.1, s32[32,128]{1,0:T(8,128)} %bitcast.9, s32[1,128]{1,0:T(1,128)} %bitcast.11, bf16[2304,512]{1,0:T(8,128)(2,1)} %bitcast.8, f32[3,3,512]{2,1,0:T(4,128)} %wd_in.1, ...), custom_call_target="tpu_custom_call" | custom-call | tf_op jit(solution)/shard_map/pallas_call | solution.py:479
  43.3 0.0 copy-done
  43.3 2.2 %shard_map.83 = bf16[8,32,512]{2,1,0:T(8,128)(2,1)} custom-call(bf16[3,256,512]{2,1,0:T(8,128)(2,1)S(1)} %get-tuple-element.8.hid0, bf16[3,288,512]{2,1,0:T(8,128)(2,1)S(1)} %get-tuple-element.9.hid1, bf16[4608,512]{1,0:T(8,128)(2,1)S(1)} %get-tuple-element.10.w2, f32[1,512]{1,0:T(1,128)S(1)} %bitcast.6), custom_call_target="tpu_custom_call" | custom-call | tf_op jit(solution)/shard_map/pallas_call | solution.py:540
Async XLA Ops:
  0.0 43.3 %copy-start = (f32[512]{0:T(512)S(1)}, f32[512]{0:T(512)}, u32[]{:S(2)}) copy-start(f32[512]{0:T(512)} %param.15) | copy-start | bytes 6148
